TPU v7x, 32 devices: a whole 2x2x4 slice. The times are simulated.
32 devices in a mesh: dp: 16 (over z, y, x), seq: 2 (over core).
Axes of the slice: x: 2, y: 2, z: 4, core: 2. Of those that a mesh axis runs over, the one named last changes fastest.
Arguments:
- layer_input: bfloat16 [16, 512, 768], P('dp', 'seq'), may hold values from -6 to 6
- encoder_states: bfloat16 [16, 3, 1500, 768], P('dp', None, 'seq'), may hold values from -6 to 6
- clip_lengths: int32 [16, 3], P('dp'), may hold values from 1 to 448, as said below
- out_grad: bfloat16 [16, 512, 768], P('dp', 'seq'), may hold values from -6 to 6
- self_weights: bfloat16 [768, 3072], P(('dp', 'seq')), may hold values from -2 to 2
- cross_weights: bfloat16 [768, 3072], P(('dp', 'seq')), may hold values from -2 to 2
- up_weights: bfloat16 [768, 3072], P(('dp', 'seq')), may hold values from -0.21875 to 0.21875
- down_weights: bfloat16 [3072, 768], P(('dp', 'seq')), may hold values from -0.15625 to 0.15625
- up_bias: bfloat16 [3072], P(('dp', 'seq')), may hold values from -3 to 3
- down_bias: bfloat16 [768], P(('dp', 'seq')), may hold values from -3 to 3
- vectors: bfloat16 [768, 12], P(('dp', 'seq')), may hold values from -2 to 2
Outputs:
- layer_output: bfloat16 [16, 512, 768], P('dp', 'seq')
- input_grad: float32 [16, 512, 768], P('dp', 'seq')
- encoder_grad: float32 [16, 3, 1500, 768], P('dp', None, 'seq')
- self_weights_grad: float32 [768, 3072], P(('dp', 'seq'))
- cross_weights_grad: float32 [768, 3072], P(('dp', 'seq'))
- up_weights_grad: float32 [768, 3072], P(('dp', 'seq'))
- down_weights_grad: float32 [3072, 768], P(('dp', 'seq'))
- up_bias_grad: float32 [3072], P(('dp', 'seq'))
- down_bias_grad: float32 [768], P(('dp', 'seq'))
- vectors_grad: float32 [768, 12], P(('dp', 'seq'))
Inputs may be any that keep to these rules, and one draw needn't show every extreme that they name: `clip_lengths`: each row's 3 clips lie end to end from the row's first token, in order, and take at most 512 tokens together; the rest of the row is padding. Every row has a clip of exactly 448 tokens.
All inputs are finite; a program needn't handle non-finite values.
Results may differ from a plain program's by a relative error of at most 0.019.
Values may be sent and summed in bfloat16 or wider, within the bound.
A program may use at most 192 MiB of HBM per device.

v0:
```python
import jax
import jax.numpy as jnp
from jax import lax
from jax.sharding import PartitionSpec as P

HEAD_DIM = 64
GROUP_HEADS = 4
CLIPS = 3


def from_behind(value, axis, steps):
    count = lax.axis_size(axis)
    leading, last = (max(0, -steps), min(count, count - steps))
    return lax.ppermute(value, axis, [(source, source + steps) for source in range(leading, last)])


def joined(array, axis, combine):
    everything = jax.tree.map(lambda part: lax.all_gather(part, axis), array)
    leading = jax.tree.map(lambda part: part[0], everything)

    def lap(k, so_far):
        return combine(so_far, jax.tree.map(lambda part: part[k], everything))

    return lax.fori_loop(1, lax.axis_size(axis), lap, leading)


def layer_norm(values, gain, shift):
    average = jnp.mean(values, -1, keepdims=True)
    centred = values - average
    spread = jnp.mean(centred * centred, -1, keepdims=True)
    return centred * lax.rsqrt(spread + 1e-05) * gain + shift


def exact_gelu(values):
    return jax.nn.gelu(values, approximate=False)


def matmul(left, right):
    return jnp.dot(left, right, preferred_element_type=jnp.float32)


def split_heads(values):
    return values.reshape(values.shape[0], -1, GROUP_HEADS, HEAD_DIM).transpose(1, 0, 2, 3)


def join_heads(values):
    return values.transpose(1, 0, 2, 3).reshape(values.shape[1], -1)


def group_scores(query_part, key_part, allowed):
    scores = (
        jnp.einsum("qhd,khd->hqk", query_part, key_part, preferred_element_type=jnp.float32) * 0.125
    )
    return jnp.where(allowed[None], scores, -1e30)


def plain_scores(query_part, key_part):
    return (
        jnp.einsum("qhd,khd->hqk", query_part, key_part, preferred_element_type=jnp.float32) * 0.125
    )


def attend_forward(queries, key_rows, value_rows, allowed):

    def one_group(operands):
        query_part, key_part, value_part = operands
        scores = group_scores(query_part, key_part, allowed)
        row_peak = jnp.max(scores, -1, keepdims=True)
        exp_terms = jnp.exp(scores - row_peak)
        row_total = jnp.sum(exp_terms, -1, keepdims=True)
        weights_low = (exp_terms / row_total).astype(jnp.bfloat16)
        result = jnp.einsum(
            "hqk,khd->qhd", weights_low, value_part, preferred_element_type=jnp.float32
        )
        return (result, (row_peak + jnp.log(row_total))[..., 0])

    return lax.map(one_group, (queries, key_rows, value_rows))


def attend_backward(queries, key_rows, value_rows, allowed, log_totals, grad_out):

    def one_group(operands):
        query_part, key_part, value_part, log_total, grad_part = operands
        scores = group_scores(query_part, key_part, allowed)
        weights = jnp.where(allowed[None], jnp.exp(scores - log_total[..., None]), 0.0)
        weights_low = weights.astype(jnp.bfloat16)
        grad_value = jnp.einsum(
            "hqk,qhd->khd", weights_low, grad_part, preferred_element_type=jnp.float32
        )
        grad_weights = jnp.einsum(
            "qhd,khd->hqk", grad_part, value_part, preferred_element_type=jnp.float32
        )
        inner = jnp.sum(grad_weights * weights, -1, keepdims=True)
        grad_scores = (weights * (grad_weights - inner)).astype(jnp.bfloat16)
        grad_query = (
            jnp.einsum("hqk,khd->qhd", grad_scores, key_part, preferred_element_type=jnp.float32)
            * 0.125
        )
        grad_key = (
            jnp.einsum("hqk,qhd->khd", grad_scores, query_part, preferred_element_type=jnp.float32)
            * 0.125
        )
        return (grad_query, grad_key, grad_value)

    return lax.map(one_group, (queries, key_rows, value_rows, log_totals, grad_out))


def local_totals(queries, key_rows):

    def one_group(operands):
        query_part, key_part = operands
        scores = plain_scores(query_part, key_part)
        row_peak = jnp.max(scores, -1)
        row_total = jnp.sum(jnp.exp(scores - row_peak[..., None]), -1)
        return (row_peak, row_total)

    return lax.map(one_group, (queries, key_rows))


def combine_totals(first, second):
    peak = jnp.maximum(first[0], second[0])
    total = first[1] * jnp.exp(first[0] - peak) + second[1] * jnp.exp(second[0] - peak)
    return (peak, total)


def partial_forward(queries, key_rows, value_rows, log_totals):

    def one_group(operands):
        query_part, key_part, value_part, log_total = operands
        scores = plain_scores(query_part, key_part)
        weights_low = jnp.exp(scores - log_total[..., None]).astype(jnp.bfloat16)
        return jnp.einsum(
            "hqk,khd->qhd", weights_low, value_part, preferred_element_type=jnp.float32
        )

    return lax.map(one_group, (queries, key_rows, value_rows, log_totals))


def partial_inner(queries, key_rows, value_rows, log_totals, grad_out):

    def one_group(operands):
        query_part, key_part, value_part, log_total, grad_part = operands
        scores = plain_scores(query_part, key_part)
        weights = jnp.exp(scores - log_total[..., None])
        grad_weights = jnp.einsum(
            "qhd,khd->hqk", grad_part, value_part, preferred_element_type=jnp.float32
        )
        return jnp.sum(grad_weights * weights, -1)

    return lax.map(one_group, (queries, key_rows, value_rows, log_totals, grad_out))


def partial_backward(queries, key_rows, value_rows, log_totals, inner_sums, grad_out):

    def one_group(operands):
        query_part, key_part, value_part, log_total, inner, grad_part = operands
        scores = plain_scores(query_part, key_part)
        weights = jnp.exp(scores - log_total[..., None])
        weights_low = weights.astype(jnp.bfloat16)
        grad_value = jnp.einsum(
            "hqk,qhd->khd", weights_low, grad_part, preferred_element_type=jnp.float32
        )
        grad_weights = jnp.einsum(
            "qhd,khd->hqk", grad_part, value_part, preferred_element_type=jnp.float32
        )
        grad_scores = (weights * (grad_weights - inner[..., None])).astype(jnp.bfloat16)
        grad_query = (
            jnp.einsum("hqk,khd->qhd", grad_scores, key_part, preferred_element_type=jnp.float32)
            * 0.125
        )
        grad_key = (
            jnp.einsum("hqk,qhd->khd", grad_scores, query_part, preferred_element_type=jnp.float32)
            * 0.125
        )
        return (grad_query, grad_key, grad_value)

    return lax.map(one_group, (queries, key_rows, value_rows, log_totals, inner_sums, grad_out))


def unpack(gathered):
    self_full, cross_full, up_full, down_full, bias_full, out_bias_full, vector_full = gathered
    return (
        self_full,
        cross_full,
        up_full,
        down_full,
        bias_full.astype(jnp.float32),
        out_bias_full.astype(jnp.float32),
        vector_full.astype(jnp.float32).T,
    )


def per_device(
    layer_input,
    encoder_states,
    clip_lengths,
    out_grad,
    self_weights,
    cross_weights,
    up_weights,
    down_weights,
    up_bias,
    down_bias,
    vectors,
):
    model_width = layer_input.shape[2]
    tok_span = layer_input.shape[1]
    seq_half = lax.axis_index("seq")
    gathered = (
        lax.all_gather(self_weights, ("dp", "seq"), axis=0, tiled=True),
        lax.all_gather(cross_weights, ("dp", "seq"), axis=0, tiled=True),
        lax.all_gather(up_weights, ("dp", "seq"), axis=0, tiled=True),
        lax.all_gather(down_weights, ("dp", "seq"), axis=0, tiled=True),
        lax.all_gather(up_bias, ("dp", "seq"), axis=0, tiled=True),
        lax.all_gather(down_bias, ("dp", "seq"), axis=0, tiled=True),
        lax.all_gather(vectors, ("dp", "seq"), axis=0, tiled=True),
    )
    self_full, cross_full, up_full, down_full, bias_full, out_bias_full, vector_full = unpack(
        gathered
    )
    source = layer_input[0].astype(jnp.float32)
    position = seq_half * tok_span + jnp.arange(tok_span, dtype=jnp.int32)
    clip_ends = jnp.cumsum(clip_lengths[0])
    segment = jnp.sum((position[:, None] >= clip_ends[None, :]).astype(jnp.int32), 1)
    key_position = jnp.concatenate([position - tok_span, position])
    key_segment = jnp.sum((key_position[:, None] >= clip_ends[None, :]).astype(jnp.int32), 1)
    allowed = (
        (key_segment[None, :] == segment[:, None])
        & (key_position[None, :] <= position[:, None])
        & (key_position[None, :] >= 0)
    )
    row_position = jnp.arange(2 * tok_span, dtype=jnp.int32)
    row_segment = jnp.sum((row_position[:, None] >= clip_ends[None, :]).astype(jnp.int32), 1)
    normed_one = layer_norm(source, vector_full[0], vector_full[1]).astype(jnp.bfloat16)
    proj_bias = jnp.concatenate([vector_full[6], jnp.zeros_like(vector_full[6]), vector_full[7]])
    qkv_low = (matmul(normed_one, self_full[:, : 3 * model_width]) + proj_bias).astype(jnp.bfloat16)
    query = qkv_low[:, :model_width]
    key_own = qkv_low[:, model_width : 2 * model_width]
    value_own = qkv_low[:, 2 * model_width :]
    key_prev, value_prev = from_behind((key_own, value_own), "seq", 1)
    key_heads = split_heads(jnp.concatenate([key_prev, key_own]))
    value_heads = split_heads(jnp.concatenate([value_prev, value_own]))
    query_heads = split_heads(query)
    attended, self_stats = attend_forward(query_heads, key_heads, value_heads, allowed)
    attended_low = join_heads(attended).astype(jnp.bfloat16)
    after_self = source + matmul(attended_low, self_full[:, 3 * model_width :]) + vector_full[8]
    normed_two = layer_norm(after_self, vector_full[2], vector_full[3]).astype(jnp.bfloat16)
    cross_query = (matmul(normed_two, cross_full[:, :model_width]) + vector_full[9]).astype(
        jnp.bfloat16
    )
    frames = encoder_states[0]
    clip_count = frames.shape[0]
    frames_here = frames.shape[1]
    flat_frames = frames.reshape(-1, model_width)
    cross_kv = matmul(flat_frames, cross_full[:, model_width : 3 * model_width])
    cross_key = (
        cross_kv[:, :model_width].astype(jnp.bfloat16).reshape(clip_count, frames_here, model_width)
    )
    cross_value = (
        (cross_kv[:, model_width:] + vector_full[10])
        .astype(jnp.bfloat16)
        .reshape(clip_count, frames_here, model_width)
    )
    cross_stats = []
    clip_keys = []
    clip_values = []
    row_query = lax.all_gather(cross_query, "seq", axis=0, tiled=True)
    cross_heads = split_heads(row_query)
    peak_list = []
    total_list = []
    for clip_index in range(CLIPS):
        clip_keys.append(split_heads(cross_key[clip_index]))
        clip_values.append(split_heads(cross_value[clip_index]))
        row_peak, row_total = local_totals(cross_heads, clip_keys[clip_index])
        peak_list.append(row_peak)
        total_list.append(row_total)
    all_peak, all_total = joined(
        (jnp.stack(peak_list), jnp.stack(total_list)), "seq", combine_totals
    )
    log_sums = all_peak + jnp.log(all_total)
    partial_value = jnp.zeros((2 * tok_span, model_width), jnp.float32)
    for clip_index in range(CLIPS):
        cross_stats.append(log_sums[clip_index])
        result = partial_forward(
            cross_heads, clip_keys[clip_index], clip_values[clip_index], log_sums[clip_index]
        )
        partial_value = partial_value + jnp.where(
            (row_segment == clip_index)[:, None], join_heads(result), 0.0
        )
    mixed = lax.psum_scatter(
        partial_value.astype(jnp.bfloat16), "seq", scatter_dimension=0, tiled=True
    )
    after_cross = after_self + matmul(mixed, cross_full[:, 3 * model_width :]) + vector_full[11]
    normed_three = layer_norm(after_cross, vector_full[4], vector_full[5]).astype(jnp.bfloat16)
    pre_act = matmul(normed_three, up_full) + bias_full
    activated_low = exact_gelu(pre_act).astype(jnp.bfloat16)
    result_rows = after_cross + matmul(activated_low, down_full) + out_bias_full
    layer_output = result_rows.astype(jnp.bfloat16)[None]
    gathered_back = (
        lax.all_gather(self_weights, ("dp", "seq"), axis=0, tiled=True),
        lax.all_gather(cross_weights, ("dp", "seq"), axis=0, tiled=True),
        lax.all_gather(up_weights, ("dp", "seq"), axis=0, tiled=True),
        lax.all_gather(down_weights, ("dp", "seq"), axis=0, tiled=True),
        lax.all_gather(up_bias, ("dp", "seq"), axis=0, tiled=True),
        lax.all_gather(down_bias, ("dp", "seq"), axis=0, tiled=True),
        lax.all_gather(vectors, ("dp", "seq"), axis=0, tiled=True),
    )
    self_back, cross_back, up_back, down_back, bias_back, _, vector_back = unpack(gathered_back)
    grad_low = out_grad[0]
    grad_rows = grad_low.astype(jnp.float32)
    grad_down = matmul(activated_low.T, grad_low)
    grad_out_bias = jnp.sum(grad_rows, 0)
    grad_act = matmul(grad_low, down_back.T).astype(jnp.bfloat16)
    _, gelu_pull = jax.vjp(exact_gelu, pre_act)
    grad_pre = gelu_pull(grad_act.astype(jnp.float32))[0].astype(jnp.bfloat16)
    grad_up = matmul(normed_three.T, grad_pre)
    grad_up_bias = jnp.sum(grad_pre, 0, dtype=jnp.float32)
    grad_normed_three = matmul(grad_pre, up_back.T)
    _, norm_pull_three = jax.vjp(layer_norm, after_cross, vector_back[4], vector_back[5])
    grad_part, grad_gain_three, grad_shift_three = norm_pull_three(grad_normed_three)
    grad_after_cross = grad_rows + grad_part
    grad_cross_low = grad_after_cross.astype(jnp.bfloat16)
    grad_cross_out = matmul(mixed.T, grad_cross_low)
    grad_cross_bias = jnp.sum(grad_cross_low, 0, dtype=jnp.float32)
    grad_mixed = matmul(grad_cross_low, cross_back[:, 3 * model_width :].T).astype(jnp.bfloat16)
    grad_keys = []
    grad_values = []
    row_grad = lax.all_gather(grad_mixed, "seq", axis=0, tiled=True)
    grad_pieces = []
    inner_list = []
    for clip_index in range(CLIPS):
        row_mask = (row_segment == clip_index)[:, None]
        grad_piece = split_heads(jnp.where(row_mask, row_grad, jnp.zeros_like(row_grad)))
        grad_pieces.append(grad_piece)
        inner_list.append(
            partial_inner(
                cross_heads,
                clip_keys[clip_index],
                clip_values[clip_index],
                cross_stats[clip_index],
                grad_piece,
            )
        )
    inner_all = lax.psum(jnp.stack(inner_list).astype(jnp.bfloat16), "seq").astype(jnp.float32)
    partial_query = jnp.zeros((2 * tok_span, model_width), jnp.float32)
    for clip_index in range(CLIPS):
        grad_query, grad_key, grad_value = partial_backward(
            cross_heads,
            clip_keys[clip_index],
            clip_values[clip_index],
            cross_stats[clip_index],
            inner_all[clip_index],
            grad_pieces[clip_index],
        )
        partial_query = partial_query + join_heads(grad_query)
        grad_keys.append(join_heads(grad_key))
        grad_values.append(join_heads(grad_value))
    grad_query_sum = lax.psum_scatter(
        partial_query.astype(jnp.bfloat16), "seq", scatter_dimension=0, tiled=True
    )
    own_key_grad = jnp.stack(grad_keys)
    own_value_grad = jnp.stack(grad_values)
    grad_cq_weight = matmul(normed_two.T, grad_query_sum)
    grad_cq_bias = jnp.sum(grad_query_sum, 0, dtype=jnp.float32)
    grad_normed_two = matmul(grad_query_sum, cross_back[:, :model_width].T)
    own_kv_low = jnp.concatenate(
        [own_key_grad.reshape(-1, model_width), own_value_grad.reshape(-1, model_width)], 1
    ).astype(jnp.bfloat16)
    grad_ckv_weight = matmul(flat_frames.T, own_kv_low)
    grad_cv_bias = jnp.sum(own_kv_low[:, model_width:], 0, dtype=jnp.float32)
    encoder_grad = matmul(own_kv_low, cross_back[:, model_width : 3 * model_width].T).reshape(
        1, clip_count, frames_here, model_width
    )
    _, norm_pull_two = jax.vjp(layer_norm, after_self, vector_back[2], vector_back[3])
    grad_part, grad_gain_two, grad_shift_two = norm_pull_two(grad_normed_two)
    grad_after_self = grad_after_cross + grad_part
    grad_self_low = grad_after_self.astype(jnp.bfloat16)
    grad_self_out = matmul(attended_low.T, grad_self_low)
    grad_self_bias = jnp.sum(grad_self_low, 0, dtype=jnp.float32)
    grad_attended = matmul(grad_self_low, self_back[:, 3 * model_width :].T).astype(jnp.bfloat16)
    grad_query, grad_key, grad_value = attend_backward(
        query_heads, key_heads, value_heads, allowed, self_stats, split_heads(grad_attended)
    )
    grad_query = join_heads(grad_query)
    grad_key = join_heads(grad_key)
    grad_value = join_heads(grad_value)
    back_key, back_value = (
        from_behind(grad_key[:tok_span].astype(jnp.bfloat16), "seq", -1).astype(jnp.float32),
        from_behind(grad_value[:tok_span].astype(jnp.bfloat16), "seq", -1).astype(jnp.float32),
    )
    grad_qkv_low = jnp.concatenate(
        [grad_query, grad_key[tok_span:] + back_key, grad_value[tok_span:] + back_value], 1
    ).astype(jnp.bfloat16)
    grad_qkv_weight = matmul(normed_one.T, grad_qkv_low)
    grad_qkv_bias = jnp.sum(grad_qkv_low, 0, dtype=jnp.float32)
    grad_normed_one = matmul(grad_qkv_low, self_back[:, : 3 * model_width].T)
    _, norm_pull_one = jax.vjp(layer_norm, source, vector_back[0], vector_back[1])
    grad_part, grad_gain_one, grad_shift_one = norm_pull_one(grad_normed_one)
    input_grad = (grad_after_self + grad_part)[None]
    grads_self = jnp.concatenate([grad_qkv_weight, grad_self_out], 1)
    grads_cross = jnp.concatenate([grad_cq_weight, grad_ckv_weight, grad_cross_out], 1)
    vector_grads = jnp.stack(
        [
            grad_gain_one,
            grad_shift_one,
            grad_gain_two,
            grad_shift_two,
            grad_gain_three,
            grad_shift_three,
            grad_qkv_bias[:model_width],
            grad_qkv_bias[2 * model_width :],
            grad_self_bias,
            grad_cq_bias,
            grad_cv_bias,
            grad_cross_bias,
        ],
        1,
    )
    shares = (
        lax.psum_scatter(grads_self, ("dp", "seq"), scatter_dimension=0, tiled=True),
        lax.psum_scatter(grads_cross, ("dp", "seq"), scatter_dimension=0, tiled=True),
        lax.psum_scatter(grad_up, ("dp", "seq"), scatter_dimension=0, tiled=True),
        lax.psum_scatter(grad_down, ("dp", "seq"), scatter_dimension=0, tiled=True),
        lax.psum_scatter(grad_up_bias, ("dp", "seq"), scatter_dimension=0, tiled=True),
        lax.psum_scatter(grad_out_bias, ("dp", "seq"), scatter_dimension=0, tiled=True),
        lax.psum_scatter(vector_grads, ("dp", "seq"), scatter_dimension=0, tiled=True),
    )
    return (
        layer_output,
        input_grad,
        encoder_grad,
        shares[0],
        shares[1],
        shares[2],
        shares[3],
        shares[4],
        shares[5],
        shares[6],
    )


def solution(mesh):
    return jax.shard_map(
        per_device,
        mesh=mesh,
        in_specs=(
            P("dp", "seq", None),
            P("dp", None, "seq", None),
            P("dp", None),
            P("dp", "seq", None),
            P(("dp", "seq"), None),
            P(("dp", "seq"), None),
            P(("dp", "seq"), None),
            P(("dp", "seq"), None),
            P(("dp", "seq")),
            P(("dp", "seq")),
            P(("dp", "seq"), None),
        ),
        out_specs=(
            P("dp", "seq", None),
            P("dp", "seq", None),
            P("dp", None, "seq", None),
            P(("dp", "seq"), None),
            P(("dp", "seq"), None),
            P(("dp", "seq"), None),
            P(("dp", "seq"), None),
            P(("dp", "seq")),
            P(("dp", "seq")),
            P(("dp", "seq"), None),
        ),
        check_vma=False,
    )
```

profile of v0, /device:TPU:0, one launch (start us, length us, event | category | flops | bytes accessed | tf_op | source)
XLA Modules:
  0.0 1169.4 jit_solution(16970273674617866992)
XLA Ops:
  8.7 44.2 %all-gather.2 = bf16[32,24,12]{1,2,0:T(8,128)(2,1)S(1)} all-gather(bf16[1,24,12]{1,2,0:T(8,128)(2,1)} %bitcast.778), channel_id=1, replica_groups=mesh['dp'=16,'seq'=2] {'dp','seq'}, dimensions={0}, use_global_device_ids=true | all-gather | bytes 19008 | tf_op jit(solution)/shard_map/all_gather | solution.py:216
  61.2 16.1 %all-gather.8.cloned.1.call-done = bf16[768,3072]{1,0:T(8,128)(2,1)} async-done(((bf16[24,3072]{1,0:T(8,128)(2,1)}), bf16[768,3072]{1,0:T(8,128)(2,1)}) %all-gather.8.cloned.1.call-update) | async-done | bytes 4718608 | tf_op jit(solution)/shard_map/all_gather | solution.py:210
  86.8 55.9 %all-gather.10.cloned.1.call-done = bf16[768,3072]{1,0:T(8,128)(2,1)} async-done(((bf16[24,3072]{1,0:T(8,128)(2,1)}), bf16[768,3072]{1,0:T(8,128)(2,1)}) %all-gather.10.cloned.1.call-update) | async-done | bytes 4718608 | tf_op jit(solution)/shard_map/all_gather | solution.py:211
  142.7 10.0 fusion.344
  178.5 16.6 %while.184 = (s32[]{:T(128)}, bf16[3,256,4,64]{1,3,2,0:T(8,128)(2,1)}, f32[3,4,256]{2,1,0:T(4,128)}, bf16[3,512,4,64]{1,3,2,0:T(8,128)(2,1)}, bf16[3,256,4,64]{1...) while((s32[]{:T(128)}, ...), condition=%wide.region_8.9_spmd.clone, body=%wide.region_5.0_spmd.clone.sunk | while | flops 141032448 | bytes 10920633 | solution.py:77
  204.7 9.3 while.174
  214.0 6.3 while.173
  232.1 10.6 while.177
  247.2 10.3 while.176
  261.9 10.3 while.175
  281.8 40.8 %all-reduce.6 = (bf16[3072]{0:T(1024)(128)(2,1)S(1)}, bf16[768]{0:T(1024)(128)(2,1)}) all-reduce(bf16[3072]{0:T(1024)(128)(2,1)S(1)} %dynamic-update-slice, bf16[768]{0:T(1024)(128)(2,1)S(1)} %dynamic-update-slice.1), channel_id=1, replica_groups=mesh['dp'=16,'seq'=2] {'dp','seq'}, use_global_device_ids=true, to_apply=%add | all-reduce | flops 3840 | bytes 15360
  327.6 26.9 %all-gather.12.cloned.1.call-done = bf16[768,3072]{1,0:T(8,128)(2,1)} async-done(((bf16[24,3072]{1,0:T(8,128)(2,1)}), bf16[768,3072]{1,0:T(8,128)(2,1)}) %all-gather.12.cloned.1.call-update) | async-done | bytes 4718608 | tf_op jit(solution)/shard_map/all_gather | solution.py:212
  354.5 11.9 %multiply_convert_fusion.4 = (bf16[256,3072]{1,0:T(8,128)(2,1)}, f32[256,3072]{1,0:T(8,128)}, f32[256,3072]{1,0:T(8,128)}) fusion(f32[3072]{0:T(1024)} %convert_element_type.182, bf16[768,3072]{1,0:T(8,128)(2,1)} %all-gather.12.cloned.1.call-done, f32[256,768]{1,0:T(8,128)} %copy-done.8, f32[768]{0:T(1024)} %get-tuple-element.760, ...), kind=kOutput, calls=%fused_computation.312 | convolution fusion | flops 1260847104 | bytes 13389824 | tf_op jit(solution)/shard_map/dot_general | solution.py:39
  366.4 53.8 %all-gather.14.cloned.1.call-done = bf16[3072,768]{1,0:T(8,128)(2,1)} async-done(((bf16[96,768]{1,0:T(8,128)(2,1)}), bf16[3072,768]{1,0:T(8,128)(2,1)}) %all-gather.14.cloned.1.call-update) | async-done | bytes 4718608 | tf_op jit(solution)/shard_map/all_gather | solution.py:213
  420.2 7.0 convert_reduce_fusion.1
  440.5 14.9 %while.180 = (s32[]{:T(128)}, bf16[3,4,512]{2,1,0:T(4,128)(2,1)S(1)}, bf16[3,512,4,64]{1,3,2,0:T(8,128)(2,1)}, bf16[3,750,4,64]{1,3,2,0:T(8,128)(2,1)}, bf16[3,5...) while((s32[]{:T(128)}, ...), condition=%wide.region_43.44_spmd, body=%wide.region_41.43_spmd.sunk | while | flops 399357952 | bytes 13654117 | solution.py:150
  457.8 11.9 %while.179 = (s32[]{:T(128)}, bf16[3,4,512]{2,1,0:T(4,128)(2,1)S(1)}, bf16[3,512,4,64]{1,3,2,0:T(8,128)(2,1)}, bf16[3,750,4,64]{1,3,2,0:T(8,128)(2,1)}, bf16[3,5...) while((s32[]{:T(128)}, ...), condition=%wide.region_40.41_spmd, body=%wide.region_38.40_spmd.sunk | while | flops 399357952 | bytes 13654117 | solution.py:150
  472.0 11.9 %while.178 = (s32[]{:T(128)}, bf16[3,4,512]{2,1,0:T(4,128)(2,1)S(1)}, bf16[3,512,4,64]{1,3,2,0:T(8,128)(2,1)}, bf16[3,750,4,64]{1,3,2,0:T(8,128)(2,1)}, bf16[3,5...) while((s32[]{:T(128)}, ...), condition=%wide.region_37.38_spmd, body=%wide.region_35.37_spmd.sunk | while | flops 399357952 | bytes 13654117 | solution.py:150
  491.5 32.3 %while.183 = (s32[]{:T(128)}, f32[3,512,4,64]{1,3,2,0:T(8,128)}, bf16[3,750,4,64]{1,3,2,0:T(8,128)(2,1)}, bf16[3,750,4,64]{1,3,2,0:T(8,128)(2,1)}, bf16[3,750,4,...) while((s32[]{:T(128)}, f32[3,512,4,64]{1,3,2,0:T(8,128)}, ...), condition=%wide.region_50.51_spmd, body=%wide.region_49.50_spmd.sunk | while | flops 995651072 | bytes 53654788 | solution.py:177
  527.4 25.9 %while.181 = (s32[]{:T(128)}, f32[3,512,4,64]{1,3,2,0:T(8,128)}, bf16[3,750,4,64]{1,3,2,0:T(8,128)(2,1)}, bf16[3,750,4,64]{1,3,2,0:T(8,128)(2,1)}, bf16[3,750,4,...) while((s32[]{:T(128)}, f32[3,512,4,64]{1,3,2,0:T(8,128)}, ...), condition=%wide.region_46.47_spmd, body=%wide.region_45.46_spmd.sunk | while | flops 995651072 | bytes 53662980 | solution.py:177
  557.0 25.9 %while.182 = (s32[]{:T(128)}, f32[3,512,4,64]{1,3,2,0:T(8,128)}, bf16[3,750,4,64]{1,3,2,0:T(8,128)(2,1)}, bf16[3,750,4,64]{1,3,2,0:T(8,128)(2,1)}, bf16[3,750,4,...) while((s32[]{:T(128)}, f32[3,512,4,64]{1,3,2,0:T(8,128)}, ...), condition=%wide.region_48.49_spmd, body=%wide.region_47.48_spmd.sunk | while | flops 995651072 | bytes 50517224 | solution.py:177
  635.9 7.5 convolution_bitcast_fusion.2
  646.5 7.4 pad_maximum_fusion.1
  653.9 9.8 copy.163
  675.2 31.3 %while.185 = (s32[]{:T(128)}, bf16[3,256,4,64]{1,3,2,0:T(8,128)(2,1)}, f32[3,512,4,64]{1,3,2,0:T(8,128)}, f32[3,512,4,64]{1,3,2,0:T(8,128)}, bf16[3,512,4,64]{1,...) while((s32[]{:T(128)}, ...), condition=%wide.region_56.57_spmd.clone, body=%wide.region_54.56_spmd.clone.sunk | while | flops 341507072 | bytes 21790416 | solution.py:105
  720.2 9.0 pad_maximum_fusion
  729.8 10.4 fusion.282
  740.2 10.7 reshape.342
  763.4 40.9 %all-reduce.5 = (f32[3072]{0:T(1024)S(1)}, f32[768]{0:T(1024)S(1)}, f32[768,12]{0,1:T(8,128)S(1)}) all-reduce(f32[3072]{0:T(1024)S(1)} %copy-done.98, f32[768]{0:T(1024)S(1)} %copy-done.90, f32[768,12]{0,1:T(8,128)S(1)} %stack.113), channel_id=10, replica_groups=mesh['dp'=16,'seq'=2] {'dp','seq'}, use_global_device_ids=true, to_apply=%region_64.65.clone | all-reduce | flops 13056 | bytes 104448
  807.4 71.8 %reduce-scatter.18.cloned.1.call-done = f32[96,768]{1,0:T(8,128)} async-done(((f32[3072,768]{1,0:T(8,128)}), f32[96,768]{1,0:T(8,128)}) %reduce-scatter.18.cloned.1.call-update) | async-done | bytes 294928 | tf_op jit(solution)/shard_map/reduce_scatter | solution.py:423
  879.1 141.4 %reduce-scatter.20.cloned.1.call-done = f32[24,3072]{1,0:T(8,128)} async-done(((f32[768,3072]{1,0:T(8,128)}), f32[24,3072]{1,0:T(8,128)}) %reduce-scatter.20.cloned.1.call-update) | async-done | bytes 294928
  1020.5 141.8 %reduce-scatter.14.cloned.1.call-done = f32[24,3072]{1,0:T(8,128)} async-done(((f32[768,3072]{1,0:T(8,128)}), f32[24,3072]{1,0:T(8,128)}) %reduce-scatter.14.cloned.1.call-update) | async-done | bytes 294928 | tf_op jit(solution)/shard_map/reduce_scatter | solution.py:420
  (689 shorter events, 440.7 us)
Async XLA Ops:
  7.2 70.1 %all-gather.8.cloned.1.call-start = ((), (), s32[]{:S(2)}) async-start(), calls=%async_computation.6 | async-start | bytes 4866048 | tf_op jit(solution)/shard_map/all_gather | solution.py:210
  7.9 134.8 %all-gather.10.cloned.1.call-start = ((), (), s32[]{:S(2)}) async-start(), calls=%async_computation.7 | async-start | bytes 4866048 | tf_op jit(solution)/shard_map/all_gather | solution.py:211
  8.7 314.5 %reduce-scatter.10.cloned.1.call-start = ((), (), s32[]{:S(2)}) async-start(), calls=%async_computation.8 | async-start | bytes 1179648 | tf_op jit(solution)/shard_map/reduce_scatter | solution.py:290
  60.0 20.5 %copy-start.66 = (f32[768]{0:T(1024)}, f32[768]{0:T(1024)S(1)}, u32[]{:S(2)}) copy-start(f32[768]{0:T(1024)S(1)} %get-tuple-element.770) | copy-start | bytes 9220
  60.0 20.5 %copy-start.74 = (f32[768]{0:T(1024)}, f32[768]{0:T(1024)S(1)}, u32[]{:S(2)}) copy-start(f32[768]{0:T(1024)S(1)} %get-tuple-element.769) | copy-start | bytes 9220
  60.0 138.7 %copy-start.79 = (f32[768]{0:T(1024)}, f32[768]{0:T(1024)S(1)}, u32[]{:S(2)}) copy-start(f32[768]{0:T(1024)S(1)} %get-tuple-element.764) | copy-start | bytes 9220
  60.0 369.5 %copy-start.70 = (f32[768]{0:T(1024)}, f32[768]{0:T(1024)S(1)}, u32[]{:S(2)}) copy-start(f32[768]{0:T(1024)S(1)} %get-tuple-element.759) | copy-start | bytes 9220
  60.3 20.2 %copy-start.81 = (f32[256]{0:T(256)}, f32[256]{0:T(256)S(1)}, u32[]{:S(2)}) copy-start(f32[256]{0:T(256)S(1)} %broadcast_multiply_fusion.2) | copy-start | bytes 3076
  60.6 19.9 %copy-start.101 = (f32[256]{0:T(256)}, f32[256]{0:T(256)S(1)}, u32[]{:S(2)}) copy-start(f32[256]{0:T(256)S(1)} %fusion.309) | copy-start | bytes 3076
  60.6 19.9 %copy-start.83 = (f32[256]{0:T(256)}, f32[256]{0:T(256)S(1)}, u32[]{:S(2)}) copy-start(f32[256]{0:T(256)S(1)} %fusion.321) | copy-start | bytes 3076
  81.5 87.5 %collective-permute-start = (bf16[256,768]{1,0:T(8,128)(2,1)}, bf16[256,768]{1,0:T(8,128)(2,1)}, u32[]{:S(2)}, u32[]{:S(2)}) collective-permute-start(bf16[256,768]{1,0:T(8,128)(2,1)} %get-tuple-element.1036), channel_id=1, source_target_pairs={{0,1},{2,3},{4,5},{6,7},{8,9},{10,11},{12,13},{14,15},{16,17},{18,... | collective-permute-start | bytes 1179656 | tf_op jit(solution)/shard_map/ppermute | solution.py:14
  84.6 88.8 %collective-permute-start.1 = (bf16[256,768]{1,0:T(8,128)(2,1)}, bf16[256,768]{1,0:T(8,128)(2,1)}, u32[]{:S(2)}, u32[]{:S(2)}) collective-permute-start(bf16[256,768]{1,0:T(8,128)(2,1)} %get-tuple-element.1034), channel_id=1, source_target_pairs={{0,1},{2,3},{4,5},{6,7},{8,9},{10,11},{12,13},{14,15},{16,17},{18,... | collective-permute-start | bytes 1179656 | tf_op jit(solution)/shard_map/ppermute | solution.py:14
  178.5 17.3 %copy-start.120 = (f32[768]{0:T(1024)S(1)}, f32[768]{0:T(1024)}, u32[]{:S(2)}) copy-start(f32[768]{0:T(1024)} %get-tuple-element.766) | copy-start | bytes 9220
  275.2 47.9 %copy-start.95 = (f32[768]{0:T(1024)S(1)}, f32[768]{0:T(1024)}, u32[]{:S(2)}) copy-start(f32[768]{0:T(1024)} %get-tuple-element.761) | copy-start | bytes 9220
  278.9 75.6 %all-gather.12.cloned.1.call-start = ((), (), s32[]{:S(2)}) async-start(), calls=%async_computation.9 | async-start | bytes 4866048 | tf_op jit(solution)/shard_map/all_gather | solution.py:212
  279.5 140.7 %all-gather.14.cloned.1.call-start = ((), (), s32[]{:S(2)}) async-start(), calls=%async_computation.10 | async-start | bytes 4866048 | tf_op jit(solution)/shard_map/all_gather | solution.py:213
  280.1 363.4 %reduce-scatter.12.cloned.1.call-start = ((), (), s32[]{:S(2)}) async-start(), calls=%async_computation.11 | async-start | bytes 1179648 | tf_op jit(solution)/shard_map/reduce_scatter | solution.py:358
  354.5 65.6 %copy-start.38 = (bf16[1,256,768]{2,1,0:T(8,128)(2,1)S(1)}, bf16[1,256,768]{2,1,0:T(8,128)(2,1)}, u32[]{:S(2)}) copy-start(bf16[1,256,768]{2,1,0:T(8,128)(2,1)} %param.42) | copy-start | bytes 1179652
  440.5 17.3 %copy-start.57 = (f32[3,4,512]{2,1,0:T(4,128)S(1)}, f32[3,4,512]{2,1,0:T(4,128)}, u32[]{:S(2)}) copy-start(f32[3,4,512]{2,1,0:T(4,128)} %copy-done.56) | copy-start | bytes 73732
  440.5 17.3 %copy-start.78 = (bf16[3,4,512]{2,1,0:T(4,128)(2,1)S(1)}, bf16[3,4,512]{2,1,0:T(4,128)(2,1)}, u32[]{:S(2)}) copy-start(bf16[3,4,512]{2,1,0:T(4,128)(2,1)} %copy.256) | copy-start | bytes 36868
  457.8 14.3 %copy-start.59 = (f32[3,4,512]{2,1,0:T(4,128)S(1)}, f32[3,4,512]{2,1,0:T(4,128)}, u32[]{:S(2)}) copy-start(f32[3,4,512]{2,1,0:T(4,128)} %copy-done.58) | copy-start | bytes 73732
  457.8 14.3 %copy-start.77 = (bf16[3,4,512]{2,1,0:T(4,128)(2,1)S(1)}, bf16[3,4,512]{2,1,0:T(4,128)(2,1)}, u32[]{:S(2)}) copy-start(bf16[3,4,512]{2,1,0:T(4,128)(2,1)} %copy.262) | copy-start | bytes 36868
  586.8 220.6 %reduce-scatter.16.cloned.1.call-start = ((), (), s32[]{:S(2)}) async-start(), calls=%async_computation.13 | async-start | bytes 9732096 | tf_op jit(solution)/shard_map/reduce_scatter | solution.py:422
  592.2 287.0 %reduce-scatter.18.cloned.1.call-start = ((), (), s32[]{:S(2)}) async-start(), calls=%async_computation.14 | async-start | bytes 9732096 | tf_op jit(solution)/shard_map/reduce_scatter | solution.py:423
  598.9 421.7 %reduce-scatter.20.cloned.1.call-start = ((), (), s32[]{:S(2)}) async-start(), calls=%async_computation.15 | async-start | bytes 9732096
  663.8 498.5 %reduce-scatter.14.cloned.1.call-start = ((), (), s32[]{:S(2)}) async-start(), calls=%async_computation.12 | async-start | bytes 9732096 | tf_op jit(solution)/shard_map/reduce_scatter | solution.py:420
  706.5 8.4 copy-start.19
  707.8 7.3 collective-permute-start.3
  710.5 4.8 collective-permute-start.2
  740.2 10.7 copy-start.116
  740.2 10.7 copy-start.115
  762.4 43.8 %copy-start.5 = (f32[256,768]{1,0:T(8,128)S(1)}, f32[256,768]{1,0:T(8,128)}, u32[]{:S(2)}) copy-start(f32[256,768]{1,0:T(8,128)} %copy-done.4) | copy-start | bytes 2359300
  (143 other events, 451.0 us)
Sparse Core Ops, SparseCore 0:
  10.9 66.3 all-gather.7
  80.2 62.4 all-gather.9
  279.0 7.0 reduce-scatter.9
  289.3 65.1 all-gather.11
  357.7 62.4 all-gather.13
  586.9 7.0 reduce-scatter.11
  600.5 136.7 reduce-scatter.15
  744.8 134.3 reduce-scatter.17
  885.6 134.8 reduce-scatter.19
  1027.8 134.4 reduce-scatter.13
where the time goes:
time: 1180 us; the launch traced here: 1170 us
  waiting for transfers between devices  510 us (43%)
  matrix products  282 us (24%)
  local copies, waits for them, and re-layouts  144 us (12%)
  blocking collectives  139 us (12%)
  other arithmetic  68.2 us (6%)
  between operations  15.7 us (1%)
    unnamed x11, waiting for transfers between devices  144 us
    reduce_scatter x1, waiting for transfers between devices, per_device(): lax.psum_scatter(grads_self, ('dp', 'seq'), scatter_dimension=0, tiled=True)  142 us
    dot_general x21, matrix products, matmul(): return jnp.dot(left, right, preferred_element_type=jnp.float32)  93.8 us
    unnamed x2, blocking collectives  81.7 us
    reduce_scatter x1, waiting for transfers between devices, per_device(): lax.psum_scatter(grad_down, ('dp', 'seq'), scatter_dimension=0, tiled=True)  71.8 us
    all_gather x1, waiting for transfers between devices, per_device(): lax.all_gather(cross_weights, ('dp', 'seq'), axis=0, tiled=True)  55.9 us
    all_gather x1, waiting for transfers between devices, per_device(): lax.all_gather(down_weights, ('dp', 'seq'), axis=0, tiled=True)  53.8 us
    dot_general x21, matrix products, one_group(): jnp.einsum('qhd,khd->hqk', grad_part, value_part, preferred_element_type=...  48.2 us
  transfers between devices with their start and end apart: 14, of which 7 were waited for; matrix products, arithmetic and copies ran while one was open for 19% of the time, Pallas kernels for 0%

commit v1 on v0

--- a/solution.py
+++ b/solution.py
@@ -1,11 +1,358 @@
+import functools
+
 import jax
 import jax.numpy as jnp
 from jax import lax
+from jax.experimental import pallas as pl
+from jax.experimental.pallas import tpu as pltpu
 from jax.sharding import PartitionSpec as P
 
 HEAD_DIM = 64
 GROUP_HEADS = 4
 CLIPS = 3
+MESH = pl.DeviceIdType.MESH
+Z = 4
+
+
+class Place:
+    def __init__(self):
+        self.dp = lax.axis_index("dp")
+        self.core = lax.axis_index("seq")
+        self.z = self.dp // 4
+        self.p = self.dp % 4
+        x, y = self.p % 2, self.p // 2
+        px, py = self.p + 1 - 2 * x, self.p + 2 - 4 * y
+        self.p_first = px * (1 - self.core) + py * self.core
+        self.p_second = py * (1 - self.core) + px * self.core
+        self.p_diag = 3 - self.p
+        base = self.z * 4
+        self.first = (base + self.p_first, self.core)
+        self.second = (base + self.p_second, self.core)
+        self.up = (lax.rem(self.dp + 4, 16), self.core)
+        self.down = (lax.rem(self.dp + 12, 16), self.core)
+        self.mate = (self.dp, 1 - self.core)
+        self.has_up = self.z < Z - 1
+        self.has_down = self.z > 0
+
+    def greet(self):
+        barrier = pltpu.get_barrier_semaphore()
+        for target in (self.mate, self.first, self.second):
+            pl.semaphore_signal(barrier, inc=1, device_id=target, device_id_type=MESH)
+
+        @pl.when(self.has_up)
+        def _():
+            pl.semaphore_signal(barrier, inc=1, device_id=self.up, device_id_type=MESH)
+
+        @pl.when(self.has_down)
+        def _():
+            pl.semaphore_signal(barrier, inc=1, device_id=self.down, device_id_type=MESH)
+
+        pl.semaphore_wait(barrier, 3 + (self.z + 3) // 4 + (6 - self.z) // 4)
+
+
+def when(cond, fn):
+    if cond is None:
+        fn()
+    else:
+        pl.when(cond)(fn)
+
+
+def both(a, b):
+    if a is None:
+        return b
+    if b is None:
+        return a
+    return jnp.logical_and(a, b)
+
+
+def gather_kernel(count, plane_first, *refs):
+    ins, outs = refs[:count], refs[count:2 * count]
+    send_sem, recv_sem, own_sem = refs[2 * count:]
+    me = Place()
+    me.greet()
+    sends = []
+
+    def block(z, p):
+        return (z * 4 + p) * 2 + me.core
+
+    def send(m, src, index, target, cond):
+        slot = len(sends)
+        copy = pltpu.make_async_remote_copy(
+            src_ref=src, dst_ref=outs[m].at[index], send_sem=send_sem.at[slot],
+            recv_sem=recv_sem.at[m, index], device_id=target, device_id_type=MESH)
+        sends.append((cond, copy))
+        when(cond, copy.start)
+
+    def arrive(m, index, cond):
+        def go():
+            pltpu.make_async_remote_copy(
+                src_ref=ins[m], dst_ref=outs[m].at[index], send_sem=send_sem.at[0],
+                recv_sem=recv_sem.at[m, index], device_id=me.mate, device_id_type=MESH).wait_recv()
+        when(cond, go)
+
+    def forward(m, z, p, targets, cond=None):
+        index = block(z, p)
+        arrive(m, index, cond)
+        for target, extra in targets:
+            send(m, outs[m].at[index], index, target, both(cond, extra))
+
+    own = block(me.z, me.p)
+    for m in range(count):
+        targets = [(me.up, me.has_up), (me.down, me.has_down), (me.first, None), (me.second, None), (me.mate, None)]
+        if m in plane_first:
+            targets = targets[2:4] + targets[:2] + targets[4:]
+        for target, cond in targets:
+            send(m, ins[m], own, target, cond)
+    for m in range(count):
+        pltpu.make_async_copy(ins[m], outs[m].at[own], own_sem.at[m]).start()
+
+    up = [(me.up, me.has_up)]
+    down = [(me.down, me.has_down)]
+    mate = [(me.mate, None)]
+    for m in plane_first:
+        forward(m, me.z, me.p_first, [(me.second, None)] + up + down + mate)
+        forward(m, me.z, me.p_second, up + down + mate)
+        forward(m, me.z, me.p_diag, up + down + mate)
+    line_first = [m for m in range(count) if m not in plane_first]
+    for d in range(1, Z + 1):
+        for m in range(count):
+            below, above = me.z - d, me.z + d
+            if d < Z:
+                if m in plane_first:
+                    for p in (me.p, me.p_first, me.p_second, me.p_diag):
+                        forward(m, below, p, up + mate, below >= 0)
+                        forward(m, above, p, down + mate, above < Z)
+                else:
+                    plane = [(me.first, None), (me.second, None)] + mate
+                    forward(m, below, me.p, up + plane, below >= 0)
+                    forward(m, above, me.p, down + plane, above < Z)
+            if m not in plane_first:
+                if d == 1:
+                    forward(m, me.z, me.p_first, [(me.second, None)] + mate)
+                else:
+                    forward(m, below + 1, me.p_first, [(me.second, None)] + mate, below + 1 >= 0)
+                    forward(m, above - 1, me.p_first, [(me.second, None)] + mate, above - 1 < Z)
+    for p in (me.p_second, me.p_diag):
+        for m in line_first:
+            for d in range(Z):
+                if d == 0:
+                    forward(m, me.z, p, mate)
+                else:
+                    forward(m, me.z - d, p, mate, me.z - d >= 0)
+                    forward(m, me.z + d, p, mate, me.z + d < Z)
+    for m in range(count):
+        pltpu.make_async_copy(ins[m], outs[m].at[own], own_sem.at[m]).wait()
+        for q in range(16):
+            arrive(m, q * 2 + 1 - me.core, None)
+    for cond, copy in sends:
+        when(cond, copy.wait_send)
+
+
+def gather_all(shards, plane_first):
+    count = len(shards)
+    any_spec = pl.BlockSpec(memory_space=pl.ANY)
+    return pl.pallas_call(
+        functools.partial(gather_kernel, count, plane_first),
+        out_shape=tuple(jax.ShapeDtypeStruct((32,) + s.shape, s.dtype) for s in shards),
+        in_specs=[any_spec] * count,
+        out_specs=tuple([any_spec] * count),
+        scratch_shapes=[
+            pltpu.SemaphoreType.DMA((80 * count,)),
+            pltpu.SemaphoreType.DMA((count, 32)),
+            pltpu.SemaphoreType.DMA((count,)),
+        ],
+        compiler_params=pltpu.CompilerParams(collective_id=0, has_side_effects=True),
+        name="gather_all",
+    )(*shards)
+
+
+def scatter_kernel(count, *refs):
+    grads, outs = refs[:count], refs[count:2 * count]
+    scratch = refs[2 * count:]
+    owns, pairs, plane_as, plane_bs, plane_cs, lines = (scratch[k * count:(k + 1) * count] for k in range(6))
+    send_sem, own_sem, pair_sem, plane_sem, line_sem = scratch[6 * count:]
+    me = Place()
+    half = me.z // 2
+    near = me.z + half * (3 - 2 * me.z)
+
+    def far(k):
+        base = (3, 2, 1 - near, near)[k]
+        return base + half * (3 - 2 * base)
+
+    order = [far(k) for k in range(4)]
+    plane = [me.p_diag, me.p_first, me.p_second, me.p]
+    mate_plane = [me.p_diag, me.p_second, me.p_first, me.p]
+    for k in range(4):
+        for m in range(count):
+            pltpu.make_async_copy(grads[m].at[:, plane[k], me.core], owns[m].at[:, plane[k]], own_sem.at[m, plane[k]]).start()
+    me.greet()
+    sends = []
+
+    def send(src, dst, sem, target, cond=None):
+        slot = len(sends)
+        copy = pltpu.make_async_remote_copy(src_ref=src, dst_ref=dst, send_sem=send_sem.at[slot], recv_sem=sem, device_id=target, device_id_type=MESH)
+        sends.append((cond, copy))
+        when(cond, copy.start)
+
+    def arrive(dst, sem, cond=None):
+        when(cond, pltpu.make_async_remote_copy(src_ref=dst, dst_ref=dst, send_sem=send_sem.at[0], recv_sem=sem, device_id=me.mate, device_id_type=MESH).wait_recv)
+
+    for k in range(4):
+        for m in range(count):
+            p = mate_plane[k]
+            send(grads[m].at[:, p, 1 - me.core], pairs[m].at[:, p], pair_sem.at[m, p], me.mate)
+
+    def paired(m, p):
+        pltpu.make_async_copy(grads[m].at[:, p, me.core], owns[m].at[:, p], own_sem.at[m, p]).wait()
+        arrive(pairs[m].at[:, p], pair_sem.at[m, p])
+
+    def add(dst, *others):
+        total = dst[...].astype(jnp.float32)
+        for other in others:
+            total = total + other[...].astype(jnp.float32)
+        dst[...] = total.astype(dst.dtype)
+
+    def steps(m):
+        own = owns[m]
+        paired(m, me.p_diag)
+        for k in range(4):
+            z = order[k]
+            add(own.at[z, me.p_diag], pairs[m].at[z, me.p_diag])
+            send(own.at[z, me.p_diag], plane_as[m].at[z], plane_sem.at[m, 0, z], me.second)
+        yield
+        paired(m, me.p_second)
+        for k in range(4):
+            z = order[k]
+            add(own.at[z, me.p_second], pairs[m].at[z, me.p_second])
+            send(own.at[z, me.p_second], plane_cs[m].at[z], plane_sem.at[m, 2, z], me.second)
+        yield
+        paired(m, me.p_first)
+        for k in range(4):
+            z = order[k]
+            arrive(plane_as[m].at[z], plane_sem.at[m, 0, z])
+            add(own.at[z, me.p_first], pairs[m].at[z, me.p_first], plane_as[m].at[z])
+            send(own.at[z, me.p_first], plane_bs[m].at[z], plane_sem.at[m, 1, z], me.first)
+        yield
+        paired(m, me.p)
+        for k in range(4):
+            z = order[k]
+            arrive(plane_bs[m].at[z], plane_sem.at[m, 1, z])
+            arrive(plane_cs[m].at[z], plane_sem.at[m, 2, z])
+            if k == 3:
+                break
+            add(own.at[z, me.p], pairs[m].at[z, me.p], plane_bs[m].at[z], plane_cs[m].at[z])
+            upward = (z - me.z + 3) // 4
+            source = me.z + 1 - 2 * upward
+            came = jnp.logical_and(source >= 0, source < Z)
+
+            def gather_in(z=z, upward=upward):
+                slot = lines[m].at[upward, z]
+                arrive(slot, line_sem.at[m, upward, z])
+                add(own.at[z, me.p], slot)
+
+            pl.when(came)(gather_in)
+            target = (lax.rem(me.dp + 12 + 8 * upward, 16), me.core)
+            send(own.at[z, me.p], lines[m].at[upward, z], line_sem.at[m, upward, z], target)
+        yield
+        z = me.z
+        total = own[z, me.p].astype(jnp.float32) + pairs[m][z, me.p].astype(jnp.float32)
+        total = total + plane_bs[m][z].astype(jnp.float32) + plane_cs[m][z].astype(jnp.float32)
+        outs[m][...] = total
+        for upward, cond in ((0, me.has_up), (1, me.has_down)):
+
+            def last(upward=upward):
+                arrive(lines[m].at[upward, z], line_sem.at[m, upward, z])
+                outs[m][...] += lines[m][upward, z].astype(jnp.float32)
+
+            pl.when(cond)(last)
+
+    running = [steps(m) for m in range(count)]
+    while running:
+        still = []
+        for step in running:
+            try:
+                next(step)
+                still.append(step)
+            except StopIteration:
+                pass
+        running = still
+    for cond, copy in sends:
+        when(cond, copy.wait_send)
+
+
+def scatter_all(grads):
+    count = len(grads)
+    shapes = [g.shape[1:] for g in grads]
+    views = [g.reshape((4, 4, 2) + s) for g, s in zip(grads, shapes)]
+
+    def vmem(*lead):
+        return [pltpu.VMEM(lead + s, g.dtype) for g, s in zip(grads, shapes)]
+
+    return pl.pallas_call(
+        functools.partial(scatter_kernel, count),
+        out_shape=tuple(jax.ShapeDtypeStruct(s, jnp.float32) for s in shapes),
+        in_specs=[pl.BlockSpec(memory_space=pl.ANY)] * count,
+        out_specs=tuple([pl.BlockSpec(memory_space=pltpu.VMEM)] * count),
+        scratch_shapes=vmem(4, 4) + vmem(4, 4) + vmem(4) + vmem(4) + vmem(4) + vmem(2, 4) + [
+            pltpu.SemaphoreType.DMA((20 * count,)),
+            pltpu.SemaphoreType.DMA((count, 4)),
+            pltpu.SemaphoreType.DMA((count, 4)),
+            pltpu.SemaphoreType.DMA((count, 3, 4)),
+            pltpu.SemaphoreType.DMA((count, 2, 4)),
+        ],
+        compiler_params=pltpu.CompilerParams(collective_id=1, has_side_effects=True, vmem_limit_bytes=60 * 2**20),
+        name="scatter_all",
+    )(*views)
+
+
+def pack_rows(up_bias, down_bias, vectors, size):
+    rows = jnp.concatenate([up_bias, down_bias, vectors], 1)
+    return jnp.pad(rows, ((0, 0), (0, size - rows.shape[1])))
+
+
+def gather_weights(self_weights, cross_weights, up_weights, down_weights, up_bias, down_bias, vectors):
+    if lax.axis_size("dp") != 16:
+        return tuple(
+            lax.all_gather(part, ("dp", "seq"), axis=0, tiled=True)
+            for part in (self_weights, cross_weights, up_weights, down_weights, up_bias, down_bias, vectors)
+        )
+    small = pack_rows(up_bias[None], down_bias[None], vectors.reshape(1, -1), 2048).reshape(16, 128)
+    whole = gather_all((self_weights, cross_weights, up_weights, down_weights, small), ())
+    rows = whole[4].reshape(32, 2048)
+    n_up, n_down = up_bias.shape[0], down_bias.shape[0]
+    n_all = n_up + n_down + vectors.size
+    return tuple(w.reshape(-1, w.shape[2]) for w in whole[:4]) + (
+        rows[:, :n_up].reshape(-1),
+        rows[:, n_up:n_up + n_down].reshape(-1),
+        rows[:, n_up + n_down:n_all].reshape(-1, vectors.shape[1]),
+    )
+
+
+def scatter_grads(grads_self, grads_cross, grad_up, grad_down, grad_up_bias, grad_out_bias, vector_grads):
+    parts = (grads_self, grads_cross, grad_up, grad_down, grad_up_bias, grad_out_bias, vector_grads)
+    if lax.axis_size("dp") != 16:
+        return tuple(lax.psum_scatter(part, ("dp", "seq"), scatter_dimension=0, tiled=True) for part in parts)
+    small = pack_rows(
+        grad_up_bias.reshape(32, -1), grad_out_bias.reshape(32, -1), vector_grads.reshape(32, -1), 1024
+    ).reshape(32, 8, 128)
+    large = tuple(g.astype(jnp.bfloat16).reshape(32, -1, g.shape[1]) for g in parts[:4])
+    whole = scatter_all(large + (small,))
+    row = whole[4].reshape(-1)
+    n_up, n_down, n_vec = (g.size // 32 for g in parts[4:])
+    return tuple(whole[:4]) + (
+        row[:n_up],
+        row[n_up:n_up + n_down],
+        row[n_up + n_down:n_up + n_down + n_vec].reshape(-1, vector_grads.shape[1]),
+    )
+
+
+def seq_scatter(value):
+    span = value.shape[0] // 2
+    half = lax.axis_index("seq")
+    mine = lax.dynamic_slice_in_dim(value, half * span, span, 0)
+    other = lax.dynamic_slice_in_dim(value, (1 - half) * span, span, 0).astype(jnp.bfloat16)
+    came = lax.ppermute(other, "seq", [(0, 1), (1, 0)])
+    return mine + came.astype(value.dtype)
 
 
 def from_behind(value, axis, steps):
@@ -178,6 +525,37 @@
 
 
 def unpack(gathered):
+    self_full, cross_full, up_full, down_full, bias_full, out_bias_full, vector_full = gathered
+    return (
+        self_full,
+        cross_full,
+        up_full,
+        down_full,
+        bias_full.astype(jnp.float32),
+        out_bias_full.astype(jnp.float32),
+        vector_full.astype(jnp.float32).T,
+    )
+
+
+def per_device(
+    layer_input,
+    encoder_states,
+    clip_lengths,
+    out_grad,
+    self_weights,
+    cross_weights,
+    up_weights,
+    down_weights,
+    up_bias,
+    down_bias,
+    vectors,
+):
+    model_width = layer_input.shape[2]
+    tok_span = layer_input.shape[1]
+    seq_half = lax.axis_index("seq")
+    gathered = gather_weights(
+        self_weights, cross_weights, up_weights, down_weights, up_bias, down_bias, vectors
+    )
     self_full, cross_full, up_full, down_full, bias_full, out_bias_full, vector_full = gathered
     return (
         self_full,
@@ -287,25 +665,20 @@
         partial_value = partial_value + jnp.where(
             (row_segment == clip_index)[:, None], join_heads(result), 0.0
         )
-    mixed = lax.psum_scatter(
-        partial_value.astype(jnp.bfloat16), "seq", scatter_dimension=0, tiled=True
-    )
+    mixed = seq_scatter(partial_value).astype(jnp.bfloat16)
     after_cross = after_self + matmul(mixed, cross_full[:, 3 * model_width :]) + vector_full[11]
     normed_three = layer_norm(after_cross, vector_full[4], vector_full[5]).astype(jnp.bfloat16)
     pre_act = matmul(normed_three, up_full) + bias_full
     activated_low = exact_gelu(pre_act).astype(jnp.bfloat16)
     result_rows = after_cross + matmul(activated_low, down_full) + out_bias_full
     layer_output = result_rows.astype(jnp.bfloat16)[None]
-    gathered_back = (
-        lax.all_gather(self_weights, ("dp", "seq"), axis=0, tiled=True),
-        lax.all_gather(cross_weights, ("dp", "seq"), axis=0, tiled=True),
-        lax.all_gather(up_weights, ("dp", "seq"), axis=0, tiled=True),
-        lax.all_gather(down_weights, ("dp", "seq"), axis=0, tiled=True),
-        lax.all_gather(up_bias, ("dp", "seq"), axis=0, tiled=True),
-        lax.all_gather(down_bias, ("dp", "seq"), axis=0, tiled=True),
-        lax.all_gather(vectors, ("dp", "seq"), axis=0, tiled=True),
-    )
-    self_back, cross_back, up_back, down_back, bias_back, _, vector_back = unpack(gathered_back)
+    self_back, cross_back, up_back, down_back, vector_back = (
+        self_full,
+        cross_full,
+        up_full,
+        down_full,
+        vector_full,
+    )
     grad_low = out_grad[0]
     grad_rows = grad_low.astype(jnp.float32)
     grad_down = matmul(activated_low.T, grad_low)
@@ -355,9 +728,7 @@
         partial_query = partial_query + join_heads(grad_query)
         grad_keys.append(join_heads(grad_key))
         grad_values.append(join_heads(grad_value))
-    grad_query_sum = lax.psum_scatter(
-        partial_query.astype(jnp.bfloat16), "seq", scatter_dimension=0, tiled=True
-    )
+    grad_query_sum = seq_scatter(partial_query).astype(jnp.bfloat16)
     own_key_grad = jnp.stack(grad_keys)
     own_value_grad = jnp.stack(grad_values)
     grad_cq_weight = matmul(normed_two.T, grad_query_sum)
@@ -416,14 +787,8 @@
         ],
         1,
     )
-    shares = (
-        lax.psum_scatter(grads_self, ("dp", "seq"), scatter_dimension=0, tiled=True),
-        lax.psum_scatter(grads_cross, ("dp", "seq"), scatter_dimension=0, tiled=True),
-        lax.psum_scatter(grad_up, ("dp", "seq"), scatter_dimension=0, tiled=True),
-        lax.psum_scatter(grad_down, ("dp", "seq"), scatter_dimension=0, tiled=True),
-        lax.psum_scatter(grad_up_bias, ("dp", "seq"), scatter_dimension=0, tiled=True),
-        lax.psum_scatter(grad_out_bias, ("dp", "seq"), scatter_dimension=0, tiled=True),
-        lax.psum_scatter(vector_grads, ("dp", "seq"), scatter_dimension=0, tiled=True),
+    shares = scatter_grads(
+        grads_self, grads_cross, grad_up, grad_down, grad_up_bias, grad_out_bias, vector_grads
     )
     return (
         layer_output,

time: 1180 us -> 819 us (0.69)
  waiting for transfers between devices: 510 us -> 71 us
  Pallas kernels: 0 us -> 105 us
  blocking collectives: 139 us -> 98 us
  local copies, waits for them, and re-layouts: 144 us -> 164 us
    reduce_scatter x5 -> x0, waiting for transfers between devices: 214 us -> none  [the longest x1 142 us: per_device(): lax.psum_scatter(grads_self, ('dp', 'seq'), scatter_dimension=0, tiled=True)]
    unnamed x11 -> x4, waiting for transfers between devices: 144 us -> 2.58 us
    pallas_call x0 -> x1, Pallas kernels: none -> 105 us  [scatter_all(): pl.pallas_call(functools.partial(scatter_kernel, count), out_shape=tuple(...]
    all_gather x1, waiting for transfers between devices: 53.8 us -> 0.01 us  [per_device(): lax.all_gather(down_weights, ('dp', 'seq'), axis=0, tiled=True)]
    unnamed x2 -> x1, blocking collectives: 81.7 us -> 40.4 us
    all_gather x1, waiting for transfers between devices: 26.9 us -> 0.01 us  [per_device(): lax.all_gather(up_weights, ('dp', 'seq'), axis=0, tiled=True)]
    unnamed x225 -> x201, local copies, waits for them, and re-layouts: 30.2 us -> 24 us
  transfers between devices with their start and end apart: 14 -> 10, of which waited for: 7 -> 2; matrix products, arithmetic and copies ran while one was open for 19% -> 33% of each run, Pallas kernels for 0% -> 0%
where the time goes in v1:
time: 819 us; the launch traced here: 811 us
  matrix products  280 us (34%)
  local copies, waits for them, and re-layouts  164 us (20%)
  Pallas kernels  105 us (13%)
  blocking collectives  98 us (12%)
  waiting for transfers between devices  71 us (9%)
  other arithmetic  67.8 us (8%)
  between operations  15.1 us (2%)
  starting transfers between devices  8.61 us (1%)
    pallas_call x1, Pallas kernels, scatter_all(): pl.pallas_call(functools.partial(scatter_kernel, count), out_shape=tuple(...  105 us
    dot_general x21, matrix products, matmul(): return jnp.dot(left, right, preferred_element_type=jnp.float32)  91.2 us
    all_gather x1, waiting for transfers between devices, per_device(): lax.all_gather(cross_weights, ('dp', 'seq'), axis=0, tiled=True)  55.8 us
    dot_general x21, matrix products, one_group(): jnp.einsum('qhd,khd->hqk', grad_part, value_part, preferred_element_type=...  48.2 us
    all_gather x1, blocking collectives, per_device(): lax.all_gather(vectors, ('dp', 'seq'), axis=0, tiled=True)  44.4 us
    dot_general x27, matrix products, plain_scores(): jnp.einsum('qhd,khd->hqk', query_part, key_part, preferred_element_type=j...  44 us
    unnamed x1, blocking collectives  40.4 us
    dot_general x12, matrix products, one_group(): jnp.einsum('hqk,khd->qhd', weights_low, value_part, preferred_element_typ...  36.6 us
  transfers between devices with their start and end apart: 10, of which 2 were waited for; matrix products, arithmetic and copies ran while one was open for 33% of the time, Pallas kernels for 0%

profile of v1, /device:TPU:0, one launch (start us, length us, event | category | flops | bytes accessed | tf_op | source)
XLA Modules:
  0.0 811.1 jit_solution(13864070387462655213)
XLA Ops:
  10.6 44.4 %all-gather.2 = bf16[32,24,12]{1,2,0:T(8,128)(2,1)S(1)} all-gather(bf16[1,24,12]{1,2,0:T(8,128)(2,1)} %bitcast.808), channel_id=1, replica_groups=mesh['dp'=16,'seq'=2] {'dp','seq'}, dimensions={0}, use_global_device_ids=true | all-gather | bytes 19008 | tf_op jit(solution)/shard_map/all_gather | solution.py:594
  59.6 4.6 reshape_squeeze.21
  64.8 12.6 %all-gather.8.cloned.1.call-done = bf16[768,3072]{1,0:T(8,128)(2,1)} async-done(((bf16[24,3072]{1,0:T(8,128)(2,1)}), bf16[768,3072]{1,0:T(8,128)(2,1)}) %all-gather.8.cloned.1.call-update) | async-done | bytes 4718608 | tf_op jit(solution)/shard_map/all_gather | solution.py:588
  87.0 55.8 %all-gather.10.cloned.1.call-done = bf16[768,3072]{1,0:T(8,128)(2,1)} async-done(((bf16[24,3072]{1,0:T(8,128)(2,1)}), bf16[768,3072]{1,0:T(8,128)(2,1)}) %all-gather.10.cloned.1.call-update) | async-done | bytes 4718608 | tf_op jit(solution)/shard_map/all_gather | solution.py:589
  142.8 10.0 %fusion.340 = (bf16[2250,1536]{1,0:T(8,128)(2,1)}, f32[2250,1536]{1,0:T(8,128)S(1)}) fusion(bf16[2250,768]{1,0:T(8,128)(2,1)} %reshape_squeeze.21, bf16[768,3072]{1,0:T(8,128)(2,1)} %all-gather.10.cloned.1.call-done), kind=kOutput, calls=%fused_computation.489 | convolution fusion | flops 5311872000 | bytes 26560512 | tf_op jit(solution)/shard_map/dot_general | solution.py:386
  178.6 16.9 %while.184 = (s32[]{:T(128)}, bf16[3,256,4,64]{1,3,2,0:T(8,128)(2,1)}, f32[3,4,256]{2,1,0:T(4,128)}, bf16[3,512,4,64]{1,3,2,0:T(8,128)(2,1)}, bf16[3,256,4,64]{1...) while((s32[]{:T(128)}, ...), condition=%wide.region_8.9_spmd.clone, body=%wide.region_5.0_spmd.clone.sunk | while | flops 141032448 | bytes 10920633 | solution.py:424
  205.4 9.3 %while.174 = (s32[]{:T(128)}, f32[3,4,512]{2,1,0:T(4,128)S(1)}, f32[3,4,512]{2,1,0:T(4,128)S(1)}, bf16[3,512,4,64]{1,3,2,0:T(8,128)(2,1)S(1)}, bf16[3,750,4,64]{1,3,2,0:T(8,128)(2,1)}, /*index=5*/s32[]{:T(128)}) while((s32[]{:T(128)}, f32[3,4,512]{2,1,0:T(4,128)S(1)}, f32[3,4,512]{2,1,0:T(4,128)S(1)}, ...), condition=%wide.region_23.24_spmd, body=%wide.region_20.23_spmd.sunk | while | flops 204283904 | bytes 13001809 | solution.py:464
  214.7 6.3 while.173
  221.0 6.3 while.172
  232.6 10.6 %while.177 = (s32[]{:T(128)}, f32[3,512,4,64]{1,3,2,0:T(8,128)}, bf16[3,750,4,64]{1,3,2,0:T(8,128)(2,1)}, bf16[3,512,4,64]{1,3,2,0:T(8,128)(2,1)S(1)}, bf16[3,75...) while((s32[]{:T(128)}, f32[3,512,4,64]{1,3,2,0:T(8,128)}, ...), condition=%wide.region_29.30_spmd, body=%wide.region_28.29_spmd.sunk | while | flops 397824000 | bytes 1599577 | solution.py:483
  247.8 10.4 %while.176 = (s32[]{:T(128)}, f32[3,512,4,64]{1,3,2,0:T(8,128)}, bf16[3,750,4,64]{1,3,2,0:T(8,128)(2,1)}, bf16[3,512,4,64]{1,3,2,0:T(8,128)(2,1)S(1)}, bf16[3,75...) while((s32[]{:T(128)}, f32[3,512,4,64]{1,3,2,0:T(8,128)}, ...), condition=%wide.region_27.28_spmd, body=%wide.region_26.27_spmd.sunk | while | flops 397824000 | bytes 1599577 | solution.py:483
  262.6 10.4 %while.175 = (s32[]{:T(128)}, f32[3,512,4,64]{1,3,2,0:T(8,128)}, bf16[3,750,4,64]{1,3,2,0:T(8,128)(2,1)}, bf16[3,512,4,64]{1,3,2,0:T(8,128)(2,1)S(1)}, bf16[3,75...) while((s32[]{:T(128)}, f32[3,512,4,64]{1,3,2,0:T(8,128)}, ...), condition=%wide.region_25.26_spmd, body=%wide.region_24.25_spmd.sunk | while | flops 397824000 | bytes 1599577 | solution.py:483
  286.3 40.4 %all-reduce.3 = (bf16[3072]{0:T(1024)(128)(2,1)}, bf16[768]{0:T(1024)(128)(2,1)}) all-reduce(bf16[3072]{0:T(1024)(128)(2,1)} %dynamic-update-slice, bf16[768]{0:T(1024)(128)(2,1)} %dynamic-update-slice.1), channel_id=1, replica_groups=mesh['dp'=16,'seq'=2] {'dp','seq'}, use_global_device_ids=true, to_apply=%add.1 | all-reduce | flops 3840 | bytes 15360
  334.9 11.8 %multiply_convert_fusion.4 = (bf16[256,3072]{1,0:T(8,128)(2,1)}, f32[256,3072]{1,0:T(8,128)}, f32[256,3072]{1,0:T(8,128)}) fusion(f32[3072]{0:T(1024)} %convert_element_type.201, bf16[768,3072]{1,0:T(8,128)(2,1)} %all-gather.12.cloned.1.call-done, f32[256,768]{1,0:T(8,128)} %copy-done.4, f32[768]{0:T(1024)} %get-tuple-element.770, ...), kind=kOutput, calls=%fused_computation.315 | convolution fusion | flops 1260847104 | bytes 13389824 | tf_op jit(solution)/shard_map/dot_general | solution.py:386
  346.8 6.9 convert_reduce_fusion.1
  371.6 14.9 %while.180 = (s32[]{:T(128)}, bf16[3,4,512]{2,1,0:T(4,128)(2,1)S(1)}, bf16[3,512,4,64]{1,3,2,0:T(8,128)(2,1)}, bf16[3,750,4,64]{1,3,2,0:T(8,128)(2,1)}, bf16[3,5...) while((s32[]{:T(128)}, ...), condition=%wide.region_42.43_spmd, body=%wide.region_40.42_spmd.sunk | while | flops 399357952 | bytes 13654117 | solution.py:497
  388.9 11.9 %while.179 = (s32[]{:T(128)}, bf16[3,4,512]{2,1,0:T(4,128)(2,1)S(1)}, bf16[3,512,4,64]{1,3,2,0:T(8,128)(2,1)}, bf16[3,750,4,64]{1,3,2,0:T(8,128)(2,1)}, bf16[3,5...) while((s32[]{:T(128)}, ...), condition=%wide.region_39.40_spmd, body=%wide.region_37.39_spmd.sunk | while | flops 399357952 | bytes 13654117 | solution.py:497
  403.2 11.9 %while.178 = (s32[]{:T(128)}, bf16[3,4,512]{2,1,0:T(4,128)(2,1)S(1)}, bf16[3,512,4,64]{1,3,2,0:T(8,128)(2,1)}, bf16[3,750,4,64]{1,3,2,0:T(8,128)(2,1)}, bf16[3,5...) while((s32[]{:T(128)}, ...), condition=%wide.region_36.37_spmd, body=%wide.region_34.36_spmd.sunk | while | flops 399357952 | bytes 13654117 | solution.py:497
  422.7 32.2 %while.183 = (s32[]{:T(128)}, f32[3,512,4,64]{1,3,2,0:T(8,128)}, bf16[3,750,4,64]{1,3,2,0:T(8,128)(2,1)}, bf16[3,750,4,64]{1,3,2,0:T(8,128)(2,1)}, bf16[3,750,4,...) while((s32[]{:T(128)}, f32[3,512,4,64]{1,3,2,0:T(8,128)}, ...), condition=%wide.region_49.50_spmd, body=%wide.region_48.49_spmd.sunk | while | flops 995651072 | bytes 53654788 | solution.py:524
  458.5 25.8 %while.181 = (s32[]{:T(128)}, f32[3,512,4,64]{1,3,2,0:T(8,128)}, bf16[3,750,4,64]{1,3,2,0:T(8,128)(2,1)}, bf16[3,750,4,64]{1,3,2,0:T(8,128)(2,1)}, bf16[3,750,4,...) while((s32[]{:T(128)}, f32[3,512,4,64]{1,3,2,0:T(8,128)}, ...), condition=%wide.region_45.46_spmd, body=%wide.region_44.45_spmd.sunk | while | flops 995651072 | bytes 53662980 | solution.py:524
  488.0 25.9 %while.182 = (s32[]{:T(128)}, f32[3,512,4,64]{1,3,2,0:T(8,128)}, bf16[3,750,4,64]{1,3,2,0:T(8,128)(2,1)}, bf16[3,750,4,64]{1,3,2,0:T(8,128)(2,1)}, bf16[3,750,4,...) while((s32[]{:T(128)}, f32[3,512,4,64]{1,3,2,0:T(8,128)}, ...), condition=%wide.region_47.48_spmd, body=%wide.region_46.47_spmd.sunk | while | flops 995651072 | bytes 50517224 | solution.py:524
  528.1 4.5 reshape.346
  532.7 4.0 constant_dynamic-update-slice_fusion.1
  547.4 4.5 reshape.347
  558.2 10.5 %convolution_convert_fusion.4 = bf16[1536,768]{0,1:T(8,128)(2,1)} fusion(bf16[2250,1536]{1,0:T(8,128)(2,1)} %constant_dynamic-update-slice_fusion, bf16[2250,768]{1,0:T(8,128)(2,1)S(1)} %copy-done.38), kind=kOutput, calls=%fused_computation.305 | convolution fusion | flops 5309595648 | bytes 12727296 | tf_op jit(solution)/shard_map/dot_general | solution.py:386
  568.7 7.8 fusion.282
  576.5 10.7 %reshape.373 = f32[1,3,750,768]{3,0,2,1:T(1,128)} reshape(f32[2250,768]{1,0:T(8,128)} %fusion.282) | data formatting | bytes 13824000 | tf_op jit(solution)/shard_map/reshape | solution.py:742
  590.3 5.1 fusion.291
  610.4 31.6 %while.185 = (s32[]{:T(128)}, bf16[3,256,4,64]{1,3,2,0:T(8,128)(2,1)}, f32[3,512,4,64]{1,3,2,0:T(8,128)}, f32[3,512,4,64]{1,3,2,0:T(8,128)}, bf16[3,512,4,64]{1,...) while((s32[]{:T(128)}, ...), condition=%wide.region_54.55_spmd.clone, body=%wide.region_52.54_spmd.clone.sunk | while | flops 341507072 | bytes 21790416 | solution.py:452
  673.6 4.1 convolution_convert_fusion.2
  681.1 7.6 pad_maximum_fusion
  688.6 105.0 %scatter_all.1 = (f32[24,3072]{1,0:T(8,128)}, f32[24,3072]{1,0:T(8,128)}, f32[24,3072]{1,0:T(8,128)}, f32[96,768]{1,0:T(8,128)}, f32[8,128]{1,0:T(8,128)}) custom-call(bf16[4,4,2,24,3072]{4,3,2,1,0:T(8,128)(2,1)} %get-tuple-element.1078.refs_0_, bf16[4,4,2,24,3072]{4,3,2,1,0:T(8,128)(2,1)} %get-tuple-element.1079.refs_1_, ...), custom_call_target="tpu_custom_call" | custom-call | tf_op jit(solution)/shard_map/scatter_all/pallas_call | solution.py:291
  (669 shorter events, 443.9 us)
Async XLA Ops:
  7.2 70.2 %all-gather.8.cloned.1.call-start = ((), (), s32[]{:S(2)}) async-start(), calls=%async_computation | async-start | bytes 4866048 | tf_op jit(solution)/shard_map/all_gather | solution.py:588
  7.9 134.9 %all-gather.10.cloned.1.call-start = ((), (), s32[]{:S(2)}) async-start(), calls=%async_computation.1 | async-start | bytes 4866048 | tf_op jit(solution)/shard_map/all_gather | solution.py:589
  8.7 326.3 %all-gather.12.cloned.1.call-start = ((), (), s32[]{:S(2)}) async-start(), calls=%async_computation.2 | async-start | bytes 4866048 | tf_op jit(solution)/shard_map/all_gather | solution.py:590
  9.4 337.4 %all-gather.14.cloned.1.call-start = ((), (), s32[]{:S(2)}) async-start(), calls=%async_computation.3 | async-start | bytes 4866048 | tf_op jit(solution)/shard_map/all_gather | solution.py:591
  56.1 21.4 %copy-start.65 = (f32[768]{0:T(1024)}, f32[768]{0:T(1024)S(1)}, u32[]{:S(2)}) copy-start(f32[768]{0:T(1024)S(1)} %get-tuple-element.780) | copy-start | bytes 9220
  56.1 21.4 %copy-start.80 = (f32[768]{0:T(1024)}, f32[768]{0:T(1024)S(1)}, u32[]{:S(2)}) copy-start(f32[768]{0:T(1024)S(1)} %get-tuple-element.779) | copy-start | bytes 9220
  56.1 143.1 %copy-start.67 = (f32[768]{0:T(1024)}, f32[768]{0:T(1024)S(1)}, u32[]{:S(2)}) copy-start(f32[768]{0:T(1024)S(1)} %get-tuple-element.774) | copy-start | bytes 9220
  57.2 20.2 %copy-start.72 = (f32[256]{0:T(256)}, f32[256]{0:T(256)S(1)}, u32[]{:S(2)}) copy-start(f32[256]{0:T(256)S(1)} %broadcast_multiply_fusion.2) | copy-start | bytes 3076
  58.6 18.8 %copy-start.85 = (f32[256]{0:T(256)}, f32[256]{0:T(256)S(1)}, u32[]{:S(2)}) copy-start(f32[256]{0:T(256)S(1)} %fusion.321) | copy-start | bytes 3076
  59.6 17.8 %copy-start.15 = (bf16[1,256,768]{2,1,0:T(8,128)(2,1)S(1)}, bf16[1,256,768]{2,1,0:T(8,128)(2,1)}, u32[]{:S(2)}) copy-start(bf16[1,256,768]{2,1,0:T(8,128)(2,1)} %param.39) | copy-start | bytes 1179652
  81.6 87.5 %collective-permute-start = (bf16[256,768]{1,0:T(8,128)(2,1)}, bf16[256,768]{1,0:T(8,128)(2,1)}, u32[]{:S(2)}, u32[]{:S(2)}) collective-permute-start(bf16[256,768]{1,0:T(8,128)(2,1)} %get-tuple-element.1045), channel_id=1, source_target_pairs={{0,1},{2,3},{4,5},{6,7},{8,9},{10,11},{12,13},{14,15},{16,17},{18,... | collective-permute-start | bytes 1179656 | tf_op jit(solution)/shard_map/ppermute | solution.py:361
  84.7 88.8 %collective-permute-start.1 = (bf16[256,768]{1,0:T(8,128)(2,1)}, bf16[256,768]{1,0:T(8,128)(2,1)}, u32[]{:S(2)}, u32[]{:S(2)}) collective-permute-start(bf16[256,768]{1,0:T(8,128)(2,1)} %get-tuple-element.1043), channel_id=1, source_target_pairs={{0,1},{2,3},{4,5},{6,7},{8,9},{10,11},{12,13},{14,15},{16,17},{18,... | collective-permute-start | bytes 1179656 | tf_op jit(solution)/shard_map/ppermute | solution.py:361
  178.6 17.7 %copy-start.108 = (f32[768]{0:T(1024)S(1)}, f32[768]{0:T(1024)}, u32[]{:S(2)}) copy-start(f32[768]{0:T(1024)} %get-tuple-element.776) | copy-start | bytes 9220
  280.8 48.4 %collective-permute-start.2 = (bf16[256,768]{1,0:T(8,128)(2,1)}, bf16[256,768]{1,0:T(8,128)(2,1)S(1)}, u32[]{:S(2)}, u32[]{:S(2)}) collective-permute-start(bf16[256,768]{1,0:T(8,128)(2,1)} %dynamic-slice_convert_fusion.1), channel_id=1, source_target_pairs={{0,1},{1,0},{2,3},{3,2},{4,5},{5,4},{6,7},{7,6},{8,9},{9,8},{10,11... | collective-permute-start | bytes 1179656 | tf_op jit(solution)/shard_map/ppermute | solution.py:354
  334.9 11.8 %copy-start.33 = (bf16[1,256,768]{2,1,0:T(8,128)(2,1)S(1)}, bf16[1,256,768]{2,1,0:T(8,128)(2,1)}, u32[]{:S(2)}) copy-start(bf16[1,256,768]{2,1,0:T(8,128)(2,1)} %param.42) | copy-start | bytes 1179652
  371.6 17.2 %copy-start.48 = (f32[3,4,512]{2,1,0:T(4,128)S(1)}, f32[3,4,512]{2,1,0:T(4,128)}, u32[]{:S(2)}) copy-start(f32[3,4,512]{2,1,0:T(4,128)} %copy-done.47) | copy-start | bytes 73732
  371.6 17.2 %copy-start.64 = (bf16[3,4,512]{2,1,0:T(4,128)(2,1)S(1)}, bf16[3,4,512]{2,1,0:T(4,128)(2,1)}, u32[]{:S(2)}) copy-start(bf16[3,4,512]{2,1,0:T(4,128)(2,1)} %copy.282) | copy-start | bytes 36868
  388.9 14.3 %copy-start.50 = (f32[3,4,512]{2,1,0:T(4,128)S(1)}, f32[3,4,512]{2,1,0:T(4,128)}, u32[]{:S(2)}) copy-start(f32[3,4,512]{2,1,0:T(4,128)} %copy-done.49) | copy-start | bytes 73732
  388.9 14.3 %copy-start.63 = (bf16[3,4,512]{2,1,0:T(4,128)(2,1)S(1)}, bf16[3,4,512]{2,1,0:T(4,128)(2,1)}, u32[]{:S(2)}) copy-start(bf16[3,4,512]{2,1,0:T(4,128)(2,1)} %copy.288) | copy-start | bytes 36868
  516.9 82.0 %collective-permute-start.3 = (bf16[256,768]{0,1:T(8,128)(2,1)S(1)}, bf16[256,768]{0,1:T(8,128)(2,1)S(1)}, u32[]{:S(2)}, u32[]{:S(2)}) collective-permute-start(bf16[256,768]{0,1:T(8,128)(2,1)S(1)} %dynamic-slice_convert_fusion), channel_id=1, source_target_pairs={{0,1},{1,0},{2,3},{3,2},{4,5},{5,4},{6,7},{7,6},{8,9},{9,8},{10,11... | collective-permute-start | bytes 1179656 | tf_op jit(solution)/shard_map/ppermute | solution.py:354
  555.0 13.7 %slice-start = ((s8[4718592]{0:T(1024)(128)(4,1)}), s8[4194304]{0:T(1024)(128)(4,1)S(1)}, s32[]{:S(2)}) async-start(s8[4718592]{0:T(1024)(128)(4,1)} %bitcast.796), calls=%async_computation.4 | async-start | bytes 8388608
  558.2 10.5 %copy-start.39 = (bf16[2250,1536]{1,0:T(8,128)(2,1)S(1)}, bf16[2250,1536]{1,0:T(8,128)(2,1)}, u32[]{:S(2)}) copy-start(bf16[2250,1536]{1,0:T(8,128)(2,1)} %constant_dynamic-update-slice_fusion) | copy-start | bytes 20736004
  558.2 10.5 %slice-start.1 = ((s8[4718592]{0:T(1024)(128)(4,1)}), s8[524288]{0:T(1024)(128)(4,1)S(1)}, s32[]{:S(2)}) async-start(s8[4718592]{0:T(1024)(128)(4,1)} %bitcast.796), calls=%async_computation.5 | async-start | bytes 1048576
  576.5 10.7 %copy-start.104 = (f32[768]{0:T(1024)S(1)}, f32[768]{0:T(1024)}, u32[]{:S(2)}) copy-start(f32[768]{0:T(1024)} %get-tuple-element.759) | copy-start | bytes 9220
  576.5 11.3 %copy-start.103 = (f32[768]{0:T(1024)S(1)}, f32[768]{0:T(1024)}, u32[]{:S(2)}) copy-start(f32[768]{0:T(1024)} %get-tuple-element.765) | copy-start | bytes 9220
  576.5 12.5 %copy-start.77 = (f32[768]{0:T(1024)S(1)}, f32[768]{0:T(1024)}, u32[]{:S(2)}) copy-start(f32[768]{0:T(1024)} %get-tuple-element.1003) | copy-start | bytes 9220
  576.5 13.1 %copy-start.84 = (f32[3072]{0:T(1024)S(1)}, f32[3072]{0:T(1024)}, u32[]{:S(2)}) copy-start(f32[3072]{0:T(1024)} %get-tuple-element.1076) | copy-start | bytes 36868
  576.5 13.8 %copy-start.6 = (f32[256,768]{1,0:T(8,128)S(1)}, f32[256,768]{1,0:T(8,128)}, u32[]{:S(2)}) copy-start(f32[256,768]{1,0:T(8,128)} %copy-done.4) | copy-start | bytes 2359300
  576.5 13.8 %copy-start.106 = (f32[768]{0:T(1024)S(1)}, f32[768]{0:T(1024)}, u32[]{:S(2)}) copy-start(f32[768]{0:T(1024)} %convert_element_type.203) | copy-start | bytes 9220
  644.3 19.4 %collective-permute-start.5 = (bf16[256,768]{1,0:T(8,128)(2,1)}, bf16[256,768]{1,0:T(8,128)(2,1)}, u32[]{:S(2)}, u32[]{:S(2)}) collective-permute-start(bf16[256,768]{1,0:T(8,128)(2,1)} %copy.177), channel_id=1, source_target_pairs={{1,0},{3,2},{5,4},{7,6},{9,8},{11,10},{13,12},{15,14},{17,16},{19,... | collective-permute-start | bytes 1179656 | tf_op jit(solution)/shard_map/ppermute | solution.py:361
  649.5 15.2 %collective-permute-start.4 = (bf16[256,768]{1,0:T(8,128)(2,1)}, bf16[256,768]{1,0:T(8,128)(2,1)}, u32[]{:S(2)}, u32[]{:S(2)}) collective-permute-start(bf16[256,768]{1,0:T(8,128)(2,1)} %copy.175), channel_id=1, source_target_pairs={{1,0},{3,2},{5,4},{7,6},{9,8},{11,10},{13,12},{15,14},{17,16},{19,... | collective-permute-start | bytes 1179656 | tf_op jit(solution)/shard_map/ppermute | solution.py:361
  656.8 9.7 %copy-start.16 = (bf16[1,256,768]{2,1,0:T(8,128)(2,1)S(1)}, bf16[1,256,768]{2,1,0:T(8,128)(2,1)}, u32[]{:S(2)}) copy-start(bf16[1,256,768]{2,1,0:T(8,128)(2,1)} %param.39) | copy-start | bytes 1179652
  (126 other events, 427.3 us)
Sparse Core Ops, SparseCore 0:
  10.9 66.4 all-gather.7
  80.3 62.4 all-gather.9
  145.7 62.4 all-gather.11
  210.9 62.5 all-gather.13

commit v2 on v1

--- a/solution.py
+++ b/solution.py
@@ -8,9 +8,206 @@
 from jax.sharding import PartitionSpec as P
 
 HEAD_DIM = 64
-GROUP_HEADS = 4
 CLIPS = 3
 MESH = pl.DeviceIdType.MESH
+NT = (((1,), (1,)), ((), ()))
+NN = (((1,), (0,)), ((), ()))
+
+
+def dot(left, right, dims):
+    return lax.dot_general(left, right, dims, preferred_element_type=jnp.float32)
+
+
+def one_head(values, h):
+    lane = lax.broadcasted_iota(jnp.int32, values.shape, 1)
+    return jnp.where((lane >= 64) == (h == 1), values, jnp.zeros_like(values))
+
+
+def self_forward_kernel(q_ref, k_ref, v_ref, bias_ref, out_ref, lse_ref):
+    keys = k_ref[...]
+    values_t = v_ref[...].T
+    halves = []
+    for h in range(2):
+        scores = dot(keys, one_head(q_ref[...], h), NT) + bias_ref[...]
+        peak = jnp.max(scores, 0, keepdims=True)
+        terms = jnp.exp(scores - peak)
+        total = jnp.sum(terms, 0, keepdims=True)
+        result = dot(values_t[h * 64:(h + 1) * 64], terms.astype(jnp.bfloat16), NN)
+        halves.append(result / total)
+        lse_ref[0, h:h + 1] = peak + jnp.log(total)
+    out_ref[...] = jnp.concatenate(halves, 0).T.astype(out_ref.dtype)
+
+
+def self_forward(q, k, v, bias):
+    toks, width = q.shape
+    keys = k.shape[0]
+    return pl.pallas_call(
+        self_forward_kernel,
+        grid=(width // 128,),
+        in_specs=[
+            pl.BlockSpec((toks, 128), lambda j: (0, j)),
+            pl.BlockSpec((keys, 128), lambda j: (0, j)),
+            pl.BlockSpec((keys, 128), lambda j: (0, j)),
+            pl.BlockSpec((keys, toks), lambda j: (0, 0)),
+        ],
+        out_specs=[
+            pl.BlockSpec((toks, 128), lambda j: (0, j)),
+            pl.BlockSpec((1, 2, toks), lambda j: (j, 0, 0)),
+        ],
+        out_shape=[
+            jax.ShapeDtypeStruct((toks, width), jnp.float32),
+            jax.ShapeDtypeStruct((width // 128, 2, toks), jnp.float32),
+        ],
+        compiler_params=pltpu.CompilerParams(vmem_limit_bytes=48 * 2**20),
+        name="self_forward",
+    )(q, k, v, bias)
+
+
+def self_backward_kernel(q_ref, k_ref, v_ref, bias_ref, lse_ref, inner_ref, g_ref, dq_ref, dk_ref, dv_ref):
+    keys, values = k_ref[...], v_ref[...]
+    keys_t = keys.T
+    grad_k = grad_v = None
+    halves = []
+    for h in range(2):
+        query, grad = one_head(q_ref[...], h), one_head(g_ref[...], h)
+        weights = jnp.exp(dot(keys, query, NT) + bias_ref[...] - lse_ref[0, h:h + 1])
+        part = dot(weights.astype(jnp.bfloat16), grad, NN)
+        grad_v = part if grad_v is None else grad_v + part
+        grad_s = (weights * (dot(values, grad, NT) - inner_ref[0, h:h + 1])).astype(jnp.bfloat16)
+        part = dot(grad_s, query, NN)
+        grad_k = part if grad_k is None else grad_k + part
+        halves.append(dot(keys_t[h * 64:(h + 1) * 64], grad_s, NN))
+    dq_ref[...] = (jnp.concatenate(halves, 0) * 0.125).T
+    dk_ref[...] = grad_k
+    dv_ref[...] = grad_v
+
+
+def self_backward(q, k, v, bias, lse, inner, grad):
+    toks, width = q.shape
+    keys = k.shape[0]
+    tok_spec = pl.BlockSpec((toks, 128), lambda j: (0, j))
+    key_spec = pl.BlockSpec((keys, 128), lambda j: (0, j))
+    row_spec = pl.BlockSpec((1, 2, toks), lambda j: (j, 0, 0))
+    return pl.pallas_call(
+        self_backward_kernel,
+        grid=(width // 128,),
+        in_specs=[tok_spec, key_spec, key_spec, pl.BlockSpec((keys, toks), lambda j: (0, 0)), row_spec, row_spec, tok_spec],
+        out_specs=[tok_spec, key_spec, key_spec],
+        out_shape=[
+            jax.ShapeDtypeStruct((toks, width), jnp.float32),
+            jax.ShapeDtypeStruct((keys, width), jnp.float32),
+            jax.ShapeDtypeStruct((keys, width), jnp.float32),
+        ],
+        compiler_params=pltpu.CompilerParams(vmem_limit_bytes=48 * 2**20),
+        name="self_backward",
+    )(q, k, v, bias, lse, inner, grad)
+
+
+def cross_forward_kernel(which, q_ref, k_ref, v_ref, seg_ref, out_ref, stat_ref, acc_ref):
+    big = which[0]
+
+    def attend(clip, values_t, query, h):
+        scores = dot(k_ref[clip], query, NT)
+        peak = jnp.max(scores, 0, keepdims=True)
+        terms = jnp.exp(scores - peak)
+        total = jnp.sum(terms, 0, keepdims=True)
+        result = dot(values_t[h * 64:(h + 1) * 64], terms.astype(jnp.bfloat16), NN)
+        return result / total, peak, total
+
+    values_t = v_ref[big].T
+    for h in range(2):
+        mine = seg_ref[...] == big
+        result, peak, total = attend(big, values_t, one_head(q_ref[...], h), h)
+        acc_ref[h * 64:(h + 1) * 64] = jnp.where(mine, result, 0.0)
+        stat_ref[0, h:h + 1] = jnp.where(mine, peak, 0.0)
+        stat_ref[0, 2 + h:3 + h] = jnp.where(mine, total, 1.0)
+    for k in (1, 2):
+        clip = which[k]
+        cols = pl.ds(pl.multiple_of(which[2 + k] * 128, 128), 128)
+        values_t = v_ref[clip].T
+        mine = seg_ref[:, cols] == clip
+        for h in range(2):
+            result, peak, total = attend(clip, values_t, one_head(q_ref[cols], h), h)
+            rows = slice(h * 64, (h + 1) * 64)
+            acc_ref[rows, cols] = jnp.where(mine, result, acc_ref[rows, cols])
+            stat_ref[0, h:h + 1, cols] = jnp.where(mine, peak, stat_ref[0, h:h + 1, cols])
+            stat_ref[0, 2 + h:3 + h, cols] = jnp.where(mine, total, stat_ref[0, 2 + h:3 + h, cols])
+    out_ref[...] = acc_ref[...].T
+
+
+def cross_forward(which, q, k, v, seg):
+    toks, width = q.shape
+    clips, frames = k.shape[:2]
+    kv_spec = pl.BlockSpec((clips, frames, 128), lambda j, w: (0, 0, j))
+    tok_spec = pl.BlockSpec((toks, 128), lambda j, w: (0, j))
+    return pl.pallas_call(
+        cross_forward_kernel,
+        grid_spec=pltpu.PrefetchScalarGridSpec(
+            num_scalar_prefetch=1,
+            grid=(width // 128,),
+            in_specs=[tok_spec, kv_spec, kv_spec, pl.BlockSpec((1, toks), lambda j, w: (0, 0))],
+            out_specs=[tok_spec, pl.BlockSpec((1, 4, toks), lambda j, w: (j, 0, 0))],
+            scratch_shapes=[pltpu.VMEM((128, toks), jnp.float32)],
+        ),
+        out_shape=[
+            jax.ShapeDtypeStruct((toks, width), jnp.float32),
+            jax.ShapeDtypeStruct((width // 128, 4, toks), jnp.float32),
+        ],
+        compiler_params=pltpu.CompilerParams(vmem_limit_bytes=48 * 2**20),
+        name="cross_forward",
+    )(which, q, k, v, seg)
+
+
+def cross_backward_kernel(which, q_ref, k_ref, v_ref, seg_ref, lse_ref, inner_ref, g_ref, dq_ref, dk_ref, dv_ref, acc_ref):
+    def back(clip, keys_t, cols, h):
+        query, grad = one_head(q_ref[cols], h), one_head(g_ref[cols], h)
+        lse = jnp.where(seg_ref[:, cols] == clip, lse_ref[0, h:h + 1, cols], 1e30)
+        weights = jnp.exp(dot(k_ref[clip], query, NT) - lse)
+        grad_v = dot(weights.astype(jnp.bfloat16), grad, NN)
+        grad_s = (weights * (dot(v_ref[clip], grad, NT) - inner_ref[0, h:h + 1, cols])).astype(jnp.bfloat16)
+        grad_k = dot(grad_s, query, NN)
+        return dot(keys_t[h * 64:(h + 1) * 64], grad_s, NN), grad_k, grad_v
+
+    for k in range(3):
+        clip = which[k]
+        cols = slice(None) if k == 0 else pl.ds(pl.multiple_of(which[2 + k] * 128, 128), 128)
+        keys_t = k_ref[clip].T
+        grad_q, grad_k, grad_v = zip(*(back(clip, keys_t, cols, h) for h in range(2)))
+        grad_q = jnp.concatenate(grad_q, 0)
+        if k == 0:
+            acc_ref[...] = grad_q
+        else:
+            acc_ref[:, cols] += grad_q
+        dk_ref[clip] = (grad_k[0] + grad_k[1]).astype(jnp.bfloat16)
+        dv_ref[clip] = (grad_v[0] + grad_v[1]).astype(jnp.bfloat16)
+    dq_ref[...] = (acc_ref[...] * 0.125).T
+
+
+def cross_backward(which, q, k, v, seg, lse, inner, grad):
+    toks, width = q.shape
+    clips, frames = k.shape[:2]
+    kv_spec = pl.BlockSpec((clips, frames, 128), lambda j, w: (0, 0, j))
+    tok_spec = pl.BlockSpec((toks, 128), lambda j, w: (0, j))
+    row_spec = pl.BlockSpec((1, 2, toks), lambda j, w: (j, 0, 0))
+    return pl.pallas_call(
+        cross_backward_kernel,
+        grid_spec=pltpu.PrefetchScalarGridSpec(
+            num_scalar_prefetch=1,
+            grid=(width // 128,),
+            in_specs=[tok_spec, kv_spec, kv_spec, pl.BlockSpec((1, toks), lambda j, w: (0, 0)), row_spec, row_spec, tok_spec],
+            out_specs=[tok_spec, kv_spec, kv_spec],
+            scratch_shapes=[pltpu.VMEM((128, toks), jnp.float32)],
+        ),
+        out_shape=[
+            jax.ShapeDtypeStruct((toks, width), jnp.float32),
+            jax.ShapeDtypeStruct(k.shape, jnp.bfloat16),
+            jax.ShapeDtypeStruct(k.shape, jnp.bfloat16),
+        ],
+        compiler_params=pltpu.CompilerParams(vmem_limit_bytes=48 * 2**20),
+        name="cross_backward",
+    )(which, q, k, v, seg, lse, inner, grad)
+
+
 Z = 4
 
 
@@ -346,29 +543,10 @@
     )
 
 
-def seq_scatter(value):
-    span = value.shape[0] // 2
-    half = lax.axis_index("seq")
-    mine = lax.dynamic_slice_in_dim(value, half * span, span, 0)
-    other = lax.dynamic_slice_in_dim(value, (1 - half) * span, span, 0).astype(jnp.bfloat16)
-    came = lax.ppermute(other, "seq", [(0, 1), (1, 0)])
-    return mine + came.astype(value.dtype)
-
-
 def from_behind(value, axis, steps):
     count = lax.axis_size(axis)
     leading, last = (max(0, -steps), min(count, count - steps))
     return lax.ppermute(value, axis, [(source, source + steps) for source in range(leading, last)])
-
-
-def joined(array, axis, combine):
-    everything = jax.tree.map(lambda part: lax.all_gather(part, axis), array)
-    leading = jax.tree.map(lambda part: part[0], everything)
-
-    def lap(k, so_far):
-        return combine(so_far, jax.tree.map(lambda part: part[k], everything))
-
-    return lax.fori_loop(1, lax.axis_size(axis), lap, leading)
 
 
 def layer_norm(values, gain, shift):
@@ -386,155 +564,31 @@
     return jnp.dot(left, right, preferred_element_type=jnp.float32)
 
 
-def split_heads(values):
-    return values.reshape(values.shape[0], -1, GROUP_HEADS, HEAD_DIM).transpose(1, 0, 2, 3)
-
-
-def join_heads(values):
-    return values.transpose(1, 0, 2, 3).reshape(values.shape[1], -1)
-
-
-def group_scores(query_part, key_part, allowed):
-    scores = (
-        jnp.einsum("qhd,khd->hqk", query_part, key_part, preferred_element_type=jnp.float32) * 0.125
-    )
-    return jnp.where(allowed[None], scores, -1e30)
-
-
-def plain_scores(query_part, key_part):
-    return (
-        jnp.einsum("qhd,khd->hqk", query_part, key_part, preferred_element_type=jnp.float32) * 0.125
-    )
-
-
-def attend_forward(queries, key_rows, value_rows, allowed):
-
-    def one_group(operands):
-        query_part, key_part, value_part = operands
-        scores = group_scores(query_part, key_part, allowed)
-        row_peak = jnp.max(scores, -1, keepdims=True)
-        exp_terms = jnp.exp(scores - row_peak)
-        row_total = jnp.sum(exp_terms, -1, keepdims=True)
-        weights_low = (exp_terms / row_total).astype(jnp.bfloat16)
-        result = jnp.einsum(
-            "hqk,khd->qhd", weights_low, value_part, preferred_element_type=jnp.float32
-        )
-        return (result, (row_peak + jnp.log(row_total))[..., 0])
-
-    return lax.map(one_group, (queries, key_rows, value_rows))
-
-
-def attend_backward(queries, key_rows, value_rows, allowed, log_totals, grad_out):
-
-    def one_group(operands):
-        query_part, key_part, value_part, log_total, grad_part = operands
-        scores = group_scores(query_part, key_part, allowed)
-        weights = jnp.where(allowed[None], jnp.exp(scores - log_total[..., None]), 0.0)
-        weights_low = weights.astype(jnp.bfloat16)
-        grad_value = jnp.einsum(
-            "hqk,qhd->khd", weights_low, grad_part, preferred_element_type=jnp.float32
-        )
-        grad_weights = jnp.einsum(
-            "qhd,khd->hqk", grad_part, value_part, preferred_element_type=jnp.float32
-        )
-        inner = jnp.sum(grad_weights * weights, -1, keepdims=True)
-        grad_scores = (weights * (grad_weights - inner)).astype(jnp.bfloat16)
-        grad_query = (
-            jnp.einsum("hqk,khd->qhd", grad_scores, key_part, preferred_element_type=jnp.float32)
-            * 0.125
-        )
-        grad_key = (
-            jnp.einsum("hqk,qhd->khd", grad_scores, query_part, preferred_element_type=jnp.float32)
-            * 0.125
-        )
-        return (grad_query, grad_key, grad_value)
-
-    return lax.map(one_group, (queries, key_rows, value_rows, log_totals, grad_out))
-
-
-def local_totals(queries, key_rows):
-
-    def one_group(operands):
-        query_part, key_part = operands
-        scores = plain_scores(query_part, key_part)
-        row_peak = jnp.max(scores, -1)
-        row_total = jnp.sum(jnp.exp(scores - row_peak[..., None]), -1)
-        return (row_peak, row_total)
-
-    return lax.map(one_group, (queries, key_rows))
-
-
-def combine_totals(first, second):
-    peak = jnp.maximum(first[0], second[0])
-    total = first[1] * jnp.exp(first[0] - peak) + second[1] * jnp.exp(second[0] - peak)
-    return (peak, total)
-
-
-def partial_forward(queries, key_rows, value_rows, log_totals):
-
-    def one_group(operands):
-        query_part, key_part, value_part, log_total = operands
-        scores = plain_scores(query_part, key_part)
-        weights_low = jnp.exp(scores - log_total[..., None]).astype(jnp.bfloat16)
-        return jnp.einsum(
-            "hqk,khd->qhd", weights_low, value_part, preferred_element_type=jnp.float32
-        )
-
-    return lax.map(one_group, (queries, key_rows, value_rows, log_totals))
-
-
-def partial_inner(queries, key_rows, value_rows, log_totals, grad_out):
-
-    def one_group(operands):
-        query_part, key_part, value_part, log_total, grad_part = operands
-        scores = plain_scores(query_part, key_part)
-        weights = jnp.exp(scores - log_total[..., None])
-        grad_weights = jnp.einsum(
-            "qhd,khd->hqk", grad_part, value_part, preferred_element_type=jnp.float32
-        )
-        return jnp.sum(grad_weights * weights, -1)
-
-    return lax.map(one_group, (queries, key_rows, value_rows, log_totals, grad_out))
-
-
-def partial_backward(queries, key_rows, value_rows, log_totals, inner_sums, grad_out):
-
-    def one_group(operands):
-        query_part, key_part, value_part, log_total, inner, grad_part = operands
-        scores = plain_scores(query_part, key_part)
-        weights = jnp.exp(scores - log_total[..., None])
-        weights_low = weights.astype(jnp.bfloat16)
-        grad_value = jnp.einsum(
-            "hqk,qhd->khd", weights_low, grad_part, preferred_element_type=jnp.float32
-        )
-        grad_weights = jnp.einsum(
-            "qhd,khd->hqk", grad_part, value_part, preferred_element_type=jnp.float32
-        )
-        grad_scores = (weights * (grad_weights - inner[..., None])).astype(jnp.bfloat16)
-        grad_query = (
-            jnp.einsum("hqk,khd->qhd", grad_scores, key_part, preferred_element_type=jnp.float32)
-            * 0.125
-        )
-        grad_key = (
-            jnp.einsum("hqk,qhd->khd", grad_scores, query_part, preferred_element_type=jnp.float32)
-            * 0.125
-        )
-        return (grad_query, grad_key, grad_value)
-
-    return lax.map(one_group, (queries, key_rows, value_rows, log_totals, inner_sums, grad_out))
-
-
-def unpack(gathered):
-    self_full, cross_full, up_full, down_full, bias_full, out_bias_full, vector_full = gathered
-    return (
-        self_full,
-        cross_full,
-        up_full,
-        down_full,
-        bias_full.astype(jnp.float32),
-        out_bias_full.astype(jnp.float32),
-        vector_full.astype(jnp.float32).T,
-    )
+def swap_halves(value):
+    return lax.ppermute(value, "seq", [(0, 1), (1, 0)])
+
+
+def seq_halves(value, axis):
+    span = value.shape[axis] // 2
+    half = lax.axis_index("seq")
+    mine = lax.dynamic_slice_in_dim(value, half * span, span, axis)
+    other = lax.dynamic_slice_in_dim(value, (1 - half) * span, span, axis)
+    return mine, other
+
+
+def seq_scatter(value):
+    mine, other = seq_halves(value, 0)
+    return mine + swap_halves(other.astype(jnp.bfloat16)).astype(value.dtype)
+
+
+def per_head(values):
+    rows = values.reshape(-1, values.shape[2]).T
+    return jnp.repeat(rows, HEAD_DIM, axis=1)
+
+
+def head_sums(values):
+    sums = jnp.sum(values.reshape(values.shape[0], -1, HEAD_DIM), -1)
+    return sums.T.reshape(-1, 2, values.shape[0])
 
 
 def per_device(
@@ -553,49 +607,14 @@
     model_width = layer_input.shape[2]
     tok_span = layer_input.shape[1]
     seq_half = lax.axis_index("seq")
-    gathered = gather_weights(
+    self_full, cross_full, up_full, down_full, bias_full, out_bias_full, vector_full = gather_weights(
         self_weights, cross_weights, up_weights, down_weights, up_bias, down_bias, vectors
     )
-    self_full, cross_full, up_full, down_full, bias_full, out_bias_full, vector_full = gathered
-    return (
-        self_full,
-        cross_full,
-        up_full,
-        down_full,
-        bias_full.astype(jnp.float32),
-        out_bias_full.astype(jnp.float32),
-        vector_full.astype(jnp.float32).T,
-    )
-
-
-def per_device(
-    layer_input,
-    encoder_states,
-    clip_lengths,
-    out_grad,
-    self_weights,
-    cross_weights,
-    up_weights,
-    down_weights,
-    up_bias,
-    down_bias,
-    vectors,
-):
-    model_width = layer_input.shape[2]
-    tok_span = layer_input.shape[1]
-    seq_half = lax.axis_index("seq")
-    gathered = (
-        lax.all_gather(self_weights, ("dp", "seq"), axis=0, tiled=True),
-        lax.all_gather(cross_weights, ("dp", "seq"), axis=0, tiled=True),
-        lax.all_gather(up_weights, ("dp", "seq"), axis=0, tiled=True),
-        lax.all_gather(down_weights, ("dp", "seq"), axis=0, tiled=True),
-        lax.all_gather(up_bias, ("dp", "seq"), axis=0, tiled=True),
-        lax.all_gather(down_bias, ("dp", "seq"), axis=0, tiled=True),
-        lax.all_gather(vectors, ("dp", "seq"), axis=0, tiled=True),
-    )
-    self_full, cross_full, up_full, down_full, bias_full, out_bias_full, vector_full = unpack(
-        gathered
-    )
+    bias_full = bias_full.astype(jnp.float32)
+    out_bias_full = out_bias_full.astype(jnp.float32)
+    vector_full = vector_full.astype(jnp.float32).T
+    cross_in = [cross_full[:, k * model_width : (k + 1) * model_width] for k in range(4)]
+
     source = layer_input[0].astype(jnp.float32)
     position = seq_half * tok_span + jnp.arange(tok_span, dtype=jnp.int32)
     clip_ends = jnp.cumsum(clip_lengths[0])
@@ -603,173 +622,133 @@
     key_position = jnp.concatenate([position - tok_span, position])
     key_segment = jnp.sum((key_position[:, None] >= clip_ends[None, :]).astype(jnp.int32), 1)
     allowed = (
-        (key_segment[None, :] == segment[:, None])
-        & (key_position[None, :] <= position[:, None])
-        & (key_position[None, :] >= 0)
-    )
+        (key_segment[:, None] == segment[None, :])
+        & (key_position[:, None] <= position[None, :])
+        & (key_position[:, None] >= 0)
+    )
+    mask_bias = jnp.where(allowed, 0.0, -1e30).astype(jnp.float32)
     row_position = jnp.arange(2 * tok_span, dtype=jnp.int32)
-    row_segment = jnp.sum((row_position[:, None] >= clip_ends[None, :]).astype(jnp.int32), 1)
+    row_segment = jnp.sum((row_position[:, None] >= clip_ends[None, :]).astype(jnp.int32), 1)[None]
+    big = jnp.argmax(clip_lengths[0]).astype(jnp.int32)
+    small_one = jnp.where(big == 0, 1, 0)
+    small_two = jnp.where(big == 2, 1, 2)
+    last_group = 2 * tok_span // 128 - 1
+    which = jnp.stack(
+        [
+            big,
+            small_one,
+            small_two,
+            jnp.where(small_one < big, 0, last_group),
+            jnp.where(small_two < big, 0, last_group),
+        ]
+    ).astype(jnp.int32)
+
     normed_one = layer_norm(source, vector_full[0], vector_full[1]).astype(jnp.bfloat16)
     proj_bias = jnp.concatenate([vector_full[6], jnp.zeros_like(vector_full[6]), vector_full[7]])
     qkv_low = (matmul(normed_one, self_full[:, : 3 * model_width]) + proj_bias).astype(jnp.bfloat16)
-    query = qkv_low[:, :model_width]
-    key_own = qkv_low[:, model_width : 2 * model_width]
-    value_own = qkv_low[:, 2 * model_width :]
-    key_prev, value_prev = from_behind((key_own, value_own), "seq", 1)
-    key_heads = split_heads(jnp.concatenate([key_prev, key_own]))
-    value_heads = split_heads(jnp.concatenate([value_prev, value_own]))
-    query_heads = split_heads(query)
-    attended, self_stats = attend_forward(query_heads, key_heads, value_heads, allowed)
-    attended_low = join_heads(attended).astype(jnp.bfloat16)
+    query = qkv_low[:, :model_width] * jnp.bfloat16(0.125)
+    kv_own = qkv_low[:, model_width:]
+    kv_row = jnp.concatenate([from_behind(kv_own, "seq", 1), kv_own])
+    key_row, value_row = kv_row[:, :model_width], kv_row[:, model_width:]
+    attended, self_lse = self_forward(query, key_row, value_row, mask_bias)
+    attended_low = attended.astype(jnp.bfloat16)
     after_self = source + matmul(attended_low, self_full[:, 3 * model_width :]) + vector_full[8]
     normed_two = layer_norm(after_self, vector_full[2], vector_full[3]).astype(jnp.bfloat16)
-    cross_query = (matmul(normed_two, cross_full[:, :model_width]) + vector_full[9]).astype(
-        jnp.bfloat16
-    )
+    cross_query = (matmul(normed_two, cross_in[0]) + vector_full[9]).astype(jnp.bfloat16)
     frames = encoder_states[0]
-    clip_count = frames.shape[0]
-    frames_here = frames.shape[1]
-    flat_frames = frames.reshape(-1, model_width)
-    cross_kv = matmul(flat_frames, cross_full[:, model_width : 3 * model_width])
-    cross_key = (
-        cross_kv[:, :model_width].astype(jnp.bfloat16).reshape(clip_count, frames_here, model_width)
-    )
+    cross_key = jnp.einsum(
+        "cfd,de->cfe", frames, cross_in[1], preferred_element_type=jnp.float32
+    ).astype(jnp.bfloat16)
     cross_value = (
-        (cross_kv[:, model_width:] + vector_full[10])
-        .astype(jnp.bfloat16)
-        .reshape(clip_count, frames_here, model_width)
-    )
-    cross_stats = []
-    clip_keys = []
-    clip_values = []
-    row_query = lax.all_gather(cross_query, "seq", axis=0, tiled=True)
-    cross_heads = split_heads(row_query)
-    peak_list = []
-    total_list = []
-    for clip_index in range(CLIPS):
-        clip_keys.append(split_heads(cross_key[clip_index]))
-        clip_values.append(split_heads(cross_value[clip_index]))
-        row_peak, row_total = local_totals(cross_heads, clip_keys[clip_index])
-        peak_list.append(row_peak)
-        total_list.append(row_total)
-    all_peak, all_total = joined(
-        (jnp.stack(peak_list), jnp.stack(total_list)), "seq", combine_totals
-    )
-    log_sums = all_peak + jnp.log(all_total)
-    partial_value = jnp.zeros((2 * tok_span, model_width), jnp.float32)
-    for clip_index in range(CLIPS):
-        cross_stats.append(log_sums[clip_index])
-        result = partial_forward(
-            cross_heads, clip_keys[clip_index], clip_values[clip_index], log_sums[clip_index]
-        )
-        partial_value = partial_value + jnp.where(
-            (row_segment == clip_index)[:, None], join_heads(result), 0.0
-        )
-    mixed = seq_scatter(partial_value).astype(jnp.bfloat16)
-    after_cross = after_self + matmul(mixed, cross_full[:, 3 * model_width :]) + vector_full[11]
+        jnp.einsum("cfd,de->cfe", frames, cross_in[2], preferred_element_type=jnp.float32)
+        + vector_full[10]
+    ).astype(jnp.bfloat16)
+    row_query = lax.all_gather(cross_query * jnp.bfloat16(0.125), "seq", axis=0, tiled=True)
+    part_mixed, part_stats = cross_forward(which, row_query, cross_key, cross_value, row_segment)
+    mixed_mine, mixed_other = seq_halves(part_mixed, 0)
+    stats_mine, stats_other = seq_halves(part_stats, 2)
+    mixed_came = swap_halves(mixed_other.astype(jnp.bfloat16))
+    stats_came = swap_halves(stats_other)
+    peak = jnp.maximum(stats_mine[:, :2], stats_came[:, :2])
+    share_mine = stats_mine[:, 2:] * jnp.exp(stats_mine[:, :2] - peak)
+    share_came = stats_came[:, 2:] * jnp.exp(stats_came[:, :2] - peak)
+    total = share_mine + share_came
+    cross_lse = peak + jnp.log(total)
+    mixed_full = mixed_mine * per_head(share_mine / total) + mixed_came.astype(
+        jnp.float32
+    ) * per_head(share_came / total)
+    mixed = mixed_full.astype(jnp.bfloat16)
+    after_cross = after_self + matmul(mixed, cross_in[3]) + vector_full[11]
     normed_three = layer_norm(after_cross, vector_full[4], vector_full[5]).astype(jnp.bfloat16)
     pre_act = matmul(normed_three, up_full) + bias_full
     activated_low = exact_gelu(pre_act).astype(jnp.bfloat16)
     result_rows = after_cross + matmul(activated_low, down_full) + out_bias_full
     layer_output = result_rows.astype(jnp.bfloat16)[None]
-    self_back, cross_back, up_back, down_back, vector_back = (
-        self_full,
-        cross_full,
-        up_full,
-        down_full,
-        vector_full,
-    )
+
     grad_low = out_grad[0]
     grad_rows = grad_low.astype(jnp.float32)
     grad_down = matmul(activated_low.T, grad_low)
     grad_out_bias = jnp.sum(grad_rows, 0)
-    grad_act = matmul(grad_low, down_back.T).astype(jnp.bfloat16)
+    grad_act = matmul(grad_low, down_full.T).astype(jnp.bfloat16)
     _, gelu_pull = jax.vjp(exact_gelu, pre_act)
     grad_pre = gelu_pull(grad_act.astype(jnp.float32))[0].astype(jnp.bfloat16)
     grad_up = matmul(normed_three.T, grad_pre)
     grad_up_bias = jnp.sum(grad_pre, 0, dtype=jnp.float32)
-    grad_normed_three = matmul(grad_pre, up_back.T)
-    _, norm_pull_three = jax.vjp(layer_norm, after_cross, vector_back[4], vector_back[5])
+    grad_normed_three = matmul(grad_pre, up_full.T)
+    _, norm_pull_three = jax.vjp(layer_norm, after_cross, vector_full[4], vector_full[5])
     grad_part, grad_gain_three, grad_shift_three = norm_pull_three(grad_normed_three)
     grad_after_cross = grad_rows + grad_part
     grad_cross_low = grad_after_cross.astype(jnp.bfloat16)
     grad_cross_out = matmul(mixed.T, grad_cross_low)
     grad_cross_bias = jnp.sum(grad_cross_low, 0, dtype=jnp.float32)
-    grad_mixed = matmul(grad_cross_low, cross_back[:, 3 * model_width :].T).astype(jnp.bfloat16)
-    grad_keys = []
-    grad_values = []
+    grad_mixed = matmul(grad_cross_low, cross_in[3].T).astype(jnp.bfloat16)
     row_grad = lax.all_gather(grad_mixed, "seq", axis=0, tiled=True)
-    grad_pieces = []
-    inner_list = []
-    for clip_index in range(CLIPS):
-        row_mask = (row_segment == clip_index)[:, None]
-        grad_piece = split_heads(jnp.where(row_mask, row_grad, jnp.zeros_like(row_grad)))
-        grad_pieces.append(grad_piece)
-        inner_list.append(
-            partial_inner(
-                cross_heads,
-                clip_keys[clip_index],
-                clip_values[clip_index],
-                cross_stats[clip_index],
-                grad_piece,
-            )
-        )
-    inner_all = lax.psum(jnp.stack(inner_list).astype(jnp.bfloat16), "seq").astype(jnp.float32)
-    partial_query = jnp.zeros((2 * tok_span, model_width), jnp.float32)
-    for clip_index in range(CLIPS):
-        grad_query, grad_key, grad_value = partial_backward(
-            cross_heads,
-            clip_keys[clip_index],
-            clip_values[clip_index],
-            cross_stats[clip_index],
-            inner_all[clip_index],
-            grad_pieces[clip_index],
-        )
-        partial_query = partial_query + join_heads(grad_query)
-        grad_keys.append(join_heads(grad_key))
-        grad_values.append(join_heads(grad_value))
-    grad_query_sum = seq_scatter(partial_query).astype(jnp.bfloat16)
-    own_key_grad = jnp.stack(grad_keys)
-    own_value_grad = jnp.stack(grad_values)
+    cross_inner = head_sums(grad_mixed.astype(jnp.float32) * mixed_full)
+    row_stats = lax.all_gather(jnp.stack([cross_lse, cross_inner]), "seq", axis=3, tiled=True)
+    part_query, grad_key, grad_value = cross_backward(
+        which, row_query, cross_key, cross_value, row_segment, row_stats[0], row_stats[1], row_grad
+    )
+    grad_query_sum = seq_scatter(part_query).astype(jnp.bfloat16)
     grad_cq_weight = matmul(normed_two.T, grad_query_sum)
     grad_cq_bias = jnp.sum(grad_query_sum, 0, dtype=jnp.float32)
-    grad_normed_two = matmul(grad_query_sum, cross_back[:, :model_width].T)
-    own_kv_low = jnp.concatenate(
-        [own_key_grad.reshape(-1, model_width), own_value_grad.reshape(-1, model_width)], 1
-    ).astype(jnp.bfloat16)
-    grad_ckv_weight = matmul(flat_frames.T, own_kv_low)
-    grad_cv_bias = jnp.sum(own_kv_low[:, model_width:], 0, dtype=jnp.float32)
-    encoder_grad = matmul(own_kv_low, cross_back[:, model_width : 3 * model_width].T).reshape(
-        1, clip_count, frames_here, model_width
-    )
-    _, norm_pull_two = jax.vjp(layer_norm, after_self, vector_back[2], vector_back[3])
+    grad_normed_two = matmul(grad_query_sum, cross_in[0].T)
+    grad_ck_weight = jnp.einsum(
+        "cfd,cfe->de", frames, grad_key, preferred_element_type=jnp.float32
+    )
+    grad_cv_weight = jnp.einsum(
+        "cfd,cfe->de", frames, grad_value, preferred_element_type=jnp.float32
+    )
+    grad_cv_bias = jnp.sum(grad_value, (0, 1), dtype=jnp.float32)
+    encoder_grad = (
+        jnp.einsum("cfe,de->cfd", grad_key, cross_in[1], preferred_element_type=jnp.float32)
+        + jnp.einsum("cfe,de->cfd", grad_value, cross_in[2], preferred_element_type=jnp.float32)
+    )[None]
+    _, norm_pull_two = jax.vjp(layer_norm, after_self, vector_full[2], vector_full[3])
     grad_part, grad_gain_two, grad_shift_two = norm_pull_two(grad_normed_two)
     grad_after_self = grad_after_cross + grad_part
     grad_self_low = grad_after_self.astype(jnp.bfloat16)
     grad_self_out = matmul(attended_low.T, grad_self_low)
     grad_self_bias = jnp.sum(grad_self_low, 0, dtype=jnp.float32)
-    grad_attended = matmul(grad_self_low, self_back[:, 3 * model_width :].T).astype(jnp.bfloat16)
-    grad_query, grad_key, grad_value = attend_backward(
-        query_heads, key_heads, value_heads, allowed, self_stats, split_heads(grad_attended)
-    )
-    grad_query = join_heads(grad_query)
-    grad_key = join_heads(grad_key)
-    grad_value = join_heads(grad_value)
-    back_key, back_value = (
-        from_behind(grad_key[:tok_span].astype(jnp.bfloat16), "seq", -1).astype(jnp.float32),
-        from_behind(grad_value[:tok_span].astype(jnp.bfloat16), "seq", -1).astype(jnp.float32),
-    )
+    grad_attended = matmul(grad_self_low, self_full[:, 3 * model_width :].T).astype(jnp.bfloat16)
+    self_inner = head_sums(grad_attended.astype(jnp.float32) * attended)
+    grad_query, grad_key_row, grad_value_row = self_backward(
+        query, key_row, value_row, mask_bias, self_lse, self_inner, grad_attended
+    )
+    grad_kv = jnp.concatenate([grad_key_row, grad_value_row], 1)
+    back_kv = from_behind(grad_kv[:tok_span].astype(jnp.bfloat16), "seq", -1)
     grad_qkv_low = jnp.concatenate(
-        [grad_query, grad_key[tok_span:] + back_key, grad_value[tok_span:] + back_value], 1
+        [grad_query, grad_kv[tok_span:] + back_kv.astype(jnp.float32)], 1
     ).astype(jnp.bfloat16)
     grad_qkv_weight = matmul(normed_one.T, grad_qkv_low)
     grad_qkv_bias = jnp.sum(grad_qkv_low, 0, dtype=jnp.float32)
-    grad_normed_one = matmul(grad_qkv_low, self_back[:, : 3 * model_width].T)
-    _, norm_pull_one = jax.vjp(layer_norm, source, vector_back[0], vector_back[1])
+    grad_normed_one = matmul(grad_qkv_low, self_full[:, : 3 * model_width].T)
+    _, norm_pull_one = jax.vjp(layer_norm, source, vector_full[0], vector_full[1])
     grad_part, grad_gain_one, grad_shift_one = norm_pull_one(grad_normed_one)
     input_grad = (grad_after_self + grad_part)[None]
     grads_self = jnp.concatenate([grad_qkv_weight, grad_self_out], 1)
-    grads_cross = jnp.concatenate([grad_cq_weight, grad_ckv_weight, grad_cross_out], 1)
+    grads_cross = jnp.concatenate(
+        [grad_cq_weight, grad_ck_weight, grad_cv_weight, grad_cross_out], 1
+    )
     vector_grads = jnp.stack(
         [
             grad_gain_one,
@@ -790,18 +769,7 @@
     shares = scatter_grads(
         grads_self, grads_cross, grad_up, grad_down, grad_up_bias, grad_out_bias, vector_grads
     )
-    return (
-        layer_output,
-        input_grad,
-        encoder_grad,
-        shares[0],
-        shares[1],
-        shares[2],
-        shares[3],
-        shares[4],
-        shares[5],
-        shares[6],
-    )
+    return (layer_output, input_grad, encoder_grad) + shares
 
 
 def solution(mesh):

time: 819 us -> 458 us (0.56)
  matrix products: 280 us -> 88.3 us
  Pallas kernels: 105 us -> 257 us
  local copies, waits for them, and re-layouts: 164 us -> 57 us
  blocking collectives: 98 us -> 7.32 us
  waiting for transfers between devices: 71 us -> 0.01 us
  other arithmetic: 67.8 us -> 31.9 us
  between operations: 15.1 us -> 4.71 us
    dot_general x102 -> x6, matrix products: 189 us -> 33.6 us  [the longest x1 7.5 us: per_device(): jnp.einsum('cfe,de->cfd', grad_value, cross_in[2], preferred_element_type...]
    pallas_call x0 -> x5, Pallas kernels: none -> 153 us  [the longest x1 88.3 us: gather_all(): pl.pallas_call(functools.partial(gather_kernel, count, plane_first), out_...]
    all_gather x4 -> x0, waiting for transfers between devices: 68.4 us -> none  [the longest x1 55.8 us: per_device(): lax.all_gather(cross_weights, ('dp', 'seq'), axis=0, tiled=True)]
    all_gather x4 -> x2, blocking collectives: 51.2 us -> 4.76 us  [the longest x1 2.89 us: per_device(): lax.all_gather(cross_query * jnp.bfloat16(0.125), 'seq', axis=0, tiled=True)]
    unnamed x1 -> x0, blocking collectives: 40.4 us -> none
    another operation x29 -> x2, local copies, waits for them, and re-layouts: 38.4 us -> 0.74 us  [the longest x1 0.73 us: per_device(): jnp.stack([big, small_one, small_two, jnp.where(small_one < big, 0, last_...]
    dot_general x21 -> x18, matrix products: 91.2 us -> 54.7 us  [matmul(): return jnp.dot(left, right, preferred_element_type=jnp.float32)]
    reshape x7 -> x6, local copies, waits for them, and re-layouts: 29.1 us -> 4.75 us  [the longest x2 4.6 us: per_head(): return jnp.repeat(rows, HEAD_DIM, axis=1)]
  transfers between devices with their start and end apart: 10 -> 5, of which waited for: 2 -> 0; matrix products, arithmetic and copies ran while one was open for 33% -> 13% of each run, Pallas kernels for 0% -> 0%
where the time goes in v2:
time: 458 us; the launch traced here: 452 us
  Pallas kernels  257 us (56%)
  matrix products  88.3 us (19%)
  local copies, waits for them, and re-layouts  57 us (12%)
  other arithmetic  31.9 us (7%)
  blocking collectives  7.32 us (2%)
  starting transfers between devices  5.68 us (1%)
  between operations  4.71 us (1%)
    pallas_call x1, Pallas kernels, scatter_all(): pl.pallas_call(functools.partial(scatter_kernel, count), out_shape=tuple(...  105 us
    pallas_call x1, Pallas kernels, gather_all(): pl.pallas_call(functools.partial(gather_kernel, count, plane_first), out_...  88.3 us
    dot_general x18, matrix products, matmul(): return jnp.dot(left, right, preferred_element_type=jnp.float32)  54.7 us
    pallas_call x1, Pallas kernels, cross_backward(): pl.pallas_call(cross_backward_kernel, grid_spec=pltpu.PrefetchScalarGridS...  28.1 us
    unnamed x180, local copies, waits for them, and re-layouts  28 us
    pallas_call x1, Pallas kernels, cross_forward(): pl.pallas_call(cross_forward_kernel, grid_spec=pltpu.PrefetchScalarGridSp...  22.1 us
  transfers between devices with their start and end apart: 5, of which 0 were waited for; matrix products, arithmetic and copies ran while one was open for 13% of the time, Pallas kernels for 0%

profile of v2, /device:TPU:0, one launch (start us, length us, event | category | flops | bytes accessed | tf_op | source)
XLA Modules:
  0.0 452.1 jit_solution(2343495688080875689)
XLA Ops:
  5.5 88.3 %gather_all.1 = (bf16[32,24,3072]{2,1,0:T(8,128)(2,1)}, bf16[32,24,3072]{2,1,0:T(8,128)(2,1)}, bf16[32,24,3072]{2,1,0:T(8,128)(2,1)}, bf16[32,96,768]{2,1,0:T(8,128)(2,1)}, bf16[32,16,128]{2,1,0:T(8,128)(2,1)}) custom-call(bf16[24,3072]{1,0:T(8,128)(2,1)} %refs_0_.1, bf16[24,3072]{1,0:T(8,128)(2,1)} %refs_1_.1, bf16[24,3072]{1,0:T(8,128)(2,1)} %refs_2_.1, ...), custom_call_target="tpu_custom_call" | custom-call | tf_op jit(solution)/shard_map/gather_all/pallas_call | solution.py:351
  96.4 6.6 %slice_reduce_fusion.1 = (f32[768]{0:T(1024)S(1)}, f32[768]{0:T(1024)S(1)}, f32[768]{0:T(1024)}, f32[768]{0:T(1024)S(1)}, f32[768]{0:T(1024)}, /*index=5*/f32[76...) fusion(f32[12,768]{0,1:T(8,128)} %bitcast.171), kind=kLoop, calls=%fused_computation.124 | loop fusion | bytes 73728 | tf_op jit(solution)/shard_map/slice | solution.py:682
  103.0 3.2 fusion.2
  108.2 3.5 collective-permute-start
  115.4 5.6 %convert_bitcast_fusion.k_ref = bf16[3,750,768]{2,1,0:T(8,128)(2,1)} fusion(bf16[1,3,750,768]{3,2,1,0:T(8,128)(2,1)S(1)} %copy-done, bf16[768,3072]{1,0:T(8,128)(2,1)} %bitcast.184), kind=kOutput, calls=%fused_computation.24 | convolution fusion | flops 2655936000 | bytes 8091648 | tf_op jit(solution)/shard_map/cfd,de->cfe/dot_general | solution.py:659
  127.3 5.5 %fusion.3.v_ref = bf16[3,750,768]{2,1,0:T(8,128)(2,1)} fusion(f32[768]{0:T(1024)S(1)} %get-tuple-element.95, bf16[1,3,750,768]{3,2,1,0:T(8,128)(2,1)S(1)} %copy-done, bf16[768,3072]{1,0:T(8,128)(2,1)} %bitcast.185), kind=kOutput, calls=%fused_computation.15 | convolution fusion | flops 2657664000 | bytes 8094720 | tf_op jit(solution)/shard_map/cfd,de->cfe/dot_general | solution.py:663
  134.5 6.7 %self_forward.1 = (f32[256,768]{1,0:T(8,128)S(1)}, f32[6,2,256]{2,1,0:T(2,128)S(1)}) custom-call(bf16[256,768]{1,0:T(8,128)(2,1)S(1)} %copy-done.13, bf16[512,768]{1,0:T(8,128)(2,1)S(1)} %get-tuple-element.122.k_ref, bf16[512,768]{1,0:T(8,128)(2,1)S(1)} %get-tuple-element.121.v_ref, f32[512,256]{1,0:T(8,128)S(1)} %copy-done.11), custom_call_target="tpu_custom_call" | custom-call | tf_op jit(solution)/shard_map/self_forward/pallas_call | solution.py:44
  146.5 2.9 all_gather.9.q_ref
  149.4 22.1 %cross_forward.1 = (f32[512,768]{1,0:T(8,128)S(1)}, f32[6,4,512]{2,1,0:T(4,128)S(1)}) custom-call(s32[5]{0:T(128)S(1)} %stack.68.which, bf16[512,768]{1,0:T(8,128)(2,1)S(1)} %all_gather.9.q_ref, bf16[3,750,768]{2,1,0:T(8,128)(2,1)S(1)} %copy-done.2, bf16[3,750,768]{2,1,0:T(8,128)(2,1)} %fusion.3.v_ref, s32[1,512]{1,0:T(1,128)S(1)} %bitcast.169), custom_call_target="tpu_custom_call" | custom-call | tf_op jit(solution)/shard_map/cross_forward/pallas_call | solution.py:143
  174.8 2.3 copy.36
  184.7 11.7 %multiply_convert_fusion = (bf16[256,3072]{1,0:T(8,128)(2,1)}, f32[256,3072]{1,0:T(8,128)S(1)}, f32[256,3072]{1,0:T(8,128)S(1)}) fusion(f32[3072]{0:T(1024)S(1)} %copy-done.62, bf16[768,3072]{1,0:T(8,128)(2,1)} %bitcast.217, f32[256,768]{1,0:T(8,128)S(1)} %get-tuple-element.135, f32[768]{0:T(1024)S(1)} %get-tuple-element.93, ...), kind=kOutput, calls=%fused_computation.28 | convolution fusion | flops 1260847104 | bytes 13389824 | tf_op jit(solution)/shard_map/dot_general | solution.py:564
  196.4 2.8 convert_reduce_fusion.1
  203.5 2.8 convert_multiply_fusion.1
  206.3 2.3 copy.37
  211.7 2.6 all_gather.11.g_ref
  215.4 28.1 %cross_backward.1 = (f32[512,768]{1,0:T(8,128)S(1)}, bf16[3,750,768]{2,1,0:T(8,128)(2,1)}, bf16[3,750,768]{2,1,0:T(8,128)(2,1)}) custom-call(s32[5]{0:T(128)S(1)} %stack.68.which, bf16[512,768]{1,0:T(8,128)(2,1)S(1)} %copy-done.4, bf16[3,750,768]{2,1,0:T(8,128)(2,1)} %convert_bitcast_fusion.k_ref, bf16[3,750,768]{2,1,0:T(8,128)(2,1)} %fusion.3.v_ref, ...), custom_call_target="tpu_custom_call" | custom-call | tf_op jit(solution)/shard_map/cross_backward/pallas_call | solution.py:192
  243.5 3.2 convert_reduce_fusion
  247.1 4.1 bitcast_convert_fusion
  251.3 3.7 convolution_convert_fusion.1
  255.0 4.2 bitcast_convert_fusion.1
  259.2 6.7 %fusion.50 = f32[3,750,768]{2,1,0:T(8,128)} fusion(bf16[3,750,768]{2,1,0:T(8,128)(2,1)S(1)} %copy-done.78, bf16[768,3072]{1,0:T(8,128)(2,1)} %bitcast.189), kind=kOutput, calls=%fused_computation.92 | convolution fusion | flops 2654208000 | bytes 11547648 | tf_op jit(solution)/shard_map/cfe,de->cfd/dot_general | solution.py:723
  266.5 7.5 %add_bitcast_fusion = f32[1,3,750,768]{3,2,1,0:T(8,128)S(1)} fusion(f32[3,750,768]{2,1,0:T(8,128)} %fusion.50, bf16[3,750,768]{2,1,0:T(8,128)(2,1)} %get-tuple-element.46, bf16[768,3072]{1,0:T(8,128)(2,1)} %bitcast.190), kind=kOutput, calls=%fused_computation.1 | convolution fusion | flops 2655936000 | bytes 18487296 | tf_op jit(solution)/shard_map/cfe,de->cfd/dot_general | solution.py:724
  274.0 9.3 %copy.41 = f32[1,3,750,768]{3,0,2,1:T(1,128)} copy(f32[1,3,750,768]{3,2,1,0:T(8,128)S(1)} %add_bitcast_fusion) | data formatting | bytes 13824000
  283.3 4.5 %fusion.36 = bf16[1,256,768]{2,1,0:T(8,128)(2,1)} fusion(f32[256,768]{1,0:T(8,128)S(1)} %copy-done.26, bf16[256,3072]{1,0:T(8,128)(2,1)S(1)} %copy-done.40, bf16[3072,768]{1,0:T(8,128)(2,1)} %bitcast.213, f32[768]{0:T(1024)S(1)} %copy-done.75), kind=kOutput, calls=%fused_computation.68 | convolution fusion | flops 1208549376 | bytes 7474176 | tf_op jit(solution)/shard_map/dot_general | solution.py:564
  287.9 3.6 convolution_convert_fusion
  295.3 3.0 convert_multiply_fusion
  298.3 2.3 copy.38
  302.9 7.5 %self_backward.1 = (f32[256,768]{1,0:T(8,128)S(1)}, f32[512,768]{1,0:T(8,128)S(1)}, f32[512,768]{1,0:T(8,128)}) custom-call(bf16[256,768]{1,0:T(8,128)(2,1)S(1)} %copy-done.14, bf16[512,768]{1,0:T(8,128)(2,1)S(1)} %copy-done.8, bf16[512,768]{1,0:T(8,128)(2,1)S(1)} %copy-done.6, f32[512,256]{1,0:T(8,128)S(1)} %copy-done.12, ...), custom_call_target="tpu_custom_call" | custom-call | tf_op jit(solution)/shard_map/self_backward/pallas_call | solution.py:91
  319.5 4.0 pad_maximum_fusion.1.refs_1_
  325.0 3.2 fusion.78
  333.8 2.8 pad_maximum_fusion.refs_0_
  336.6 104.5 %scatter_all.1 = (f32[24,3072]{1,0:T(8,128)}, f32[24,3072]{1,0:T(8,128)}, f32[24,3072]{1,0:T(8,128)}, f32[96,768]{1,0:T(8,128)}, f32[8,128]{1,0:T(8,128)}) custom-call(bf16[4,4,2,24,3072]{4,3,2,1,0:T(8,128)(2,1)} %pad_maximum_fusion.refs_0_, bf16[4,4,2,24,3072]{4,3,2,1,0:T(8,128)(2,1)} %pad_maximum_fusion.1.refs_1_, bf16[4,4,2,24,3072]{4,3,2,1,0:T(8,128)(2,1)} %bitcast.173, ...), custom_call_target="tpu_custom_call" | custom-call | tf_op jit(solution)/shard_map/scatter_all/pallas_call | solution.py:488
  (292 shorter events, 76.5 us)
Async XLA Ops:
  0.6 114.7 %copy-start = (bf16[1,3,750,768]{3,2,1,0:T(8,128)(2,1)S(1)}, bf16[1,3,750,768]{3,2,1,0:T(8,128)(2,1)}, u32[]{:S(2)}) copy-start(bf16[1,3,750,768]{3,2,1,0:T(8,128)(2,1)} %param.12) | copy-start | bytes 10368004
  1.9 101.1 %copy-start.58 = (f32[256]{0:T(256)}, f32[256]{0:T(256)S(1)}, u32[]{:S(2)}) copy-start(f32[256]{0:T(256)S(1)} %broadcast_multiply_fusion.2) | copy-start | bytes 3076
  3.2 103.0 %copy-start.68 = (f32[256]{0:T(256)}, f32[256]{0:T(256)S(1)}, u32[]{:S(2)}) copy-start(f32[256]{0:T(256)S(1)} %fusion.56) | copy-start | bytes 3076
  3.2 103.0 %copy-start.64 = (f32[256]{0:T(256)}, f32[256]{0:T(256)S(1)}, u32[]{:S(2)}) copy-start(f32[256]{0:T(256)S(1)} %fusion.68) | copy-start | bytes 3076
  103.0 41.2 %copy-start.51 = (f32[768]{0:T(1024)}, f32[768]{0:T(1024)S(1)}, u32[]{:S(2)}) copy-start(f32[768]{0:T(1024)S(1)} %get-tuple-element.98) | copy-start | bytes 9220
  103.0 41.3 %copy-start.55 = (f32[768]{0:T(1024)}, f32[768]{0:T(1024)S(1)}, u32[]{:S(2)}) copy-start(f32[768]{0:T(1024)S(1)} %get-tuple-element.97) | copy-start | bytes 9220
  103.0 12.0 %copy-start.79 = (s32[1,3]{1,0:T(1,128)S(1)}, s32[1,3]{1,0:T(1,128)}, u32[]{:S(2)}) copy-start(s32[1,3]{1,0:T(1,128)} %param.13) | copy-start | bytes 40
  108.2 24.7 %collective-permute-start = (bf16[256,1536]{1,0:T(8,128)(2,1)}, bf16[256,1536]{1,0:T(8,128)(2,1)}, u32[]{:S(2)}, u32[]{:S(2)}) collective-permute-start(bf16[256,1536]{1,0:T(8,128)(2,1)} %slice.167), channel_id=1, source_target_pairs={{0,1},{2,3},{4,5},{6,7},{8,9},{10,11},{12,13},{14,15},{16,17},{18,... | collective-permute-start | bytes 2359304 | tf_op jit(solution)/shard_map/ppermute | solution.py:549
  132.9 9.2 %copy-start.30 = (bf16[1,256,768]{2,1,0:T(8,128)(2,1)S(1)}, bf16[1,256,768]{2,1,0:T(8,128)(2,1)}, u32[]{:S(2)}) copy-start(bf16[1,256,768]{2,1,0:T(8,128)(2,1)} %param.11) | copy-start | bytes 1179652
  134.5 6.8 %copy-start.5 = (bf16[512,768]{1,0:T(8,128)(2,1)}, bf16[512,768]{1,0:T(8,128)(2,1)S(1)}, u32[]{:S(2)}) copy-start(bf16[512,768]{1,0:T(8,128)(2,1)S(1)} %get-tuple-element.121.v_ref) | copy-start | bytes 2359300
  134.5 6.8 %copy-start.7 = (bf16[512,768]{1,0:T(8,128)(2,1)}, bf16[512,768]{1,0:T(8,128)(2,1)S(1)}, u32[]{:S(2)}) copy-start(bf16[512,768]{1,0:T(8,128)(2,1)S(1)} %get-tuple-element.122.k_ref) | copy-start | bytes 2359300
  134.5 9.7 %copy-start.74 = (f32[768]{0:T(1024)S(1)}, f32[768]{0:T(1024)}, u32[]{:S(2)}) copy-start(f32[768]{0:T(1024)} %get-tuple-element.96) | copy-start | bytes 9220
  144.0 27.6 %copy-start.60 = (f32[256]{0:T(256)}, f32[256]{0:T(256)S(1)}, u32[]{:S(2)}) copy-start(f32[256]{0:T(256)S(1)} %broadcast_multiply_fusion.1) | copy-start | bytes 3076
  144.2 27.3 %copy-start.70 = (f32[256]{0:T(256)}, f32[256]{0:T(256)S(1)}, u32[]{:S(2)}) copy-start(f32[256]{0:T(256)S(1)} %multiply_reduce_fusion.5) | copy-start | bytes 3076
  144.2 27.3 %copy-start.66 = (f32[256]{0:T(256)}, f32[256]{0:T(256)S(1)}, u32[]{:S(2)}) copy-start(f32[256]{0:T(256)S(1)} %fusion.69) | copy-start | bytes 3076
  149.4 22.1 %copy-start.3 = (bf16[512,768]{1,0:T(8,128)(2,1)}, bf16[512,768]{1,0:T(8,128)(2,1)S(1)}, u32[]{:S(2)}) copy-start(bf16[512,768]{1,0:T(8,128)(2,1)S(1)} %all_gather.9.q_ref) | copy-start | bytes 2359300
  171.6 2.1 collective-permute-start.1
  173.5 6.9 %collective-permute-start.2 = (bf16[256,768]{1,0:T(8,128)(2,1)}, bf16[256,768]{1,0:T(8,128)(2,1)}, u32[]{:S(2)}, u32[]{:S(2)}) collective-permute-start(bf16[256,768]{1,0:T(8,128)(2,1)} %dynamic-slice_convert_fusion.1), channel_id=1, source_target_pairs={{0,1},{1,0},{2,3},{3,2},{4,5},{5,4},{6,7},{7,6},{8,9},{9,8},{10,11... | collective-permute-start | bytes 1179656 | tf_op jit(solution)/shard_map/ppermute | solution.py:568
  182.4 14.0 %slice-start = ((s8[4718592]{0:T(1024)(128)(4,1)}), s8[4194304]{0:T(1024)(128)(4,1)S(1)}, s32[]{:S(2)}) async-start(s8[4718592]{0:T(1024)(128)(4,1)} %bitcast.214), calls=%async_computation | async-start | bytes 8388608
  182.4 16.8 %slice-start.2 = ((s8[4718592]{0:T(1024)(128)(4,1)}), s8[4194304]{0:T(1024)(128)(4,1)S(1)}, s32[]{:S(2)}) async-start(s8[4718592]{0:T(1024)(128)(4,1)} %bitcast.218), calls=%async_computation.2 | async-start | bytes 8388608
  184.4 17.0 %copy-start.24 = (f32[256,768]{1,0:T(8,128)}, f32[256,768]{1,0:T(8,128)S(1)}, u32[]{:S(2)}) copy-start(f32[256,768]{1,0:T(8,128)S(1)} %get-tuple-element.135) | copy-start | bytes 2359300
  184.7 11.7 %copy-start.38 = (bf16[1,256,768]{2,1,0:T(8,128)(2,1)S(1)}, bf16[1,256,768]{2,1,0:T(8,128)(2,1)}, u32[]{:S(2)}) copy-start(bf16[1,256,768]{2,1,0:T(8,128)(2,1)} %param.14) | copy-start | bytes 1179652
  184.7 11.7 %slice-start.1 = ((s8[4718592]{0:T(1024)(128)(4,1)}), s8[524288]{0:T(1024)(128)(4,1)S(1)}, s32[]{:S(2)}) async-start(s8[4718592]{0:T(1024)(128)(4,1)} %bitcast.214), calls=%async_computation.1 | async-start | bytes 1048576
  184.7 14.5 %slice-start.3 = ((s8[4718592]{0:T(1024)(128)(4,1)}), s8[524288]{0:T(1024)(128)(4,1)S(1)}, s32[]{:S(2)}) async-start(s8[4718592]{0:T(1024)(128)(4,1)} %bitcast.218), calls=%async_computation.3 | async-start | bytes 1048576
  243.5 7.7 %copy-start.16 = (f32[512,768]{1,0:T(8,128)}, f32[512,768]{1,0:T(8,128)S(1)}, u32[]{:S(2)}) copy-start(f32[512,768]{1,0:T(8,128)S(1)} %get-tuple-element.40) | copy-start | bytes 4718596
  259.2 6.8 %copy-start.17 = (f32[512,768]{1,0:T(8,128)S(1)}, f32[512,768]{1,0:T(8,128)}, u32[]{:S(2)}) copy-start(f32[512,768]{1,0:T(8,128)} %copy-done.16) | copy-start | bytes 4718596
  266.1 25.4 %collective-permute-start.3 = (bf16[256,768]{1,0:T(8,128)(2,1)S(1)}, bf16[256,768]{1,0:T(8,128)(2,1)S(1)}, u32[]{:S(2)}, u32[]{:S(2)}) collective-permute-start(bf16[256,768]{1,0:T(8,128)(2,1)S(1)} %dynamic-slice_convert_fusion), channel_id=1, source_target_pairs={{0,1},{1,0},{2,3},{3,2},{4,5},{5,4},{6,7},{7,6},{8,9},{9,8},{10,11... | collective-permute-start | bytes 1179656 | tf_op jit(solution)/shard_map/ppermute | solution.py:568
  274.0 9.3 %copy-start.26 = (f32[256,768]{1,0:T(8,128)S(1)}, f32[256,768]{1,0:T(8,128)}, u32[]{:S(2)}) copy-start(f32[256,768]{1,0:T(8,128)} %copy-done.24) | copy-start | bytes 2359300
  274.0 9.3 %copy-start.40 = (bf16[256,3072]{1,0:T(8,128)(2,1)S(1)}, bf16[256,3072]{1,0:T(8,128)(2,1)}, u32[]{:S(2)}) copy-start(bf16[256,3072]{1,0:T(8,128)(2,1)} %get-tuple-element.119) | copy-start | bytes 4718596
  274.0 9.3 %copy-start.75 = (f32[768]{0:T(1024)S(1)}, f32[768]{0:T(1024)}, u32[]{:S(2)}) copy-start(f32[768]{0:T(1024)} %reshape.278) | copy-start | bytes 9220
  313.3 10.3 %collective-permute-start.4 = (bf16[256,1536]{1,0:T(8,128)(2,1)}, bf16[256,1536]{1,0:T(8,128)(2,1)}, u32[]{:S(2)}, u32[]{:S(2)}) collective-permute-start(bf16[256,1536]{1,0:T(8,128)(2,1)} %slice.246), channel_id=1, source_target_pairs={{1,0},{3,2},{5,4},{7,6},{9,8},{11,10},{13,12},{15,14},{17,16},{19,... | collective-permute-start | bytes 2359304 | tf_op jit(solution)/shard_map/ppermute | solution.py:549
  336.6 115.3 %copy-start.1 = (bf16[1,3,750,768]{3,2,1,0:T(8,128)(2,1)S(1)}, bf16[1,3,750,768]{3,2,1,0:T(8,128)(2,1)}, u32[]{:S(2)}) copy-start(bf16[1,3,750,768]{3,2,1,0:T(8,128)(2,1)} %param.12) | copy-start | bytes 10368004
  (58 other events, 208.5 us)
